TPU v7x, 32 devices: a whole 2x2x4 slice. The times are simulated.
32 devices in a mesh: curve: 16 (over z, y, core), chan: 2 (over x).
Axes of the slice: x: 2, y: 2, z: 4, core: 2. Of those that a mesh axis runs over, the one named last changes fastest.
Arguments:
- features: bfloat16 [65536, 256], P('curve', 'chan'), may hold values from -6 to 6
- cotangent: bfloat16 [65536, 256], P('curve', 'chan'), may hold values from -6 to 6
- near_kernel: bfloat16 [512, 8, 128, 128], P('curve'), may hold values from -0.1875 to 0.1875
- near_index: int32 [512, 8], P('curve'), may hold values from 0 to 511, as said below
- near_count: int32 [512], P('curve'), may hold values from 1 to 8, as said below
- basis_in: bfloat16 [512, 16, 128], P('curve'), may hold values from -0.09375 to 0.09375
- basis_out: bfloat16 [512, 128, 16], P('curve'), may hold values from -1.5 to 1.5
- far_kernel: float32 [16, 8, 16, 16], P('curve'), may hold values from -0.5 to 0.5
- far_index: int32 [16, 8], P('curve'), may hold values from 0 to 15, as said below
- channel_mix: float32 [256, 256], replicated, may hold values from -0.375 to 0.375
Outputs:
- layer_out: bfloat16 [65536, 256], P('curve', 'chan')
- feature_grad: bfloat16 [65536, 256], P('curve', 'chan')
Inputs may be any that keep to these rules, and one draw needn't show every extreme that they name: `near_index`: slot 0 of block b holds b; every slot of block b holds a block from b - 32 to b. `near_count`: in every group of 32 blocks one block has all 8 slots live and another block has one. `far_index`: every partner of group g differs from g by 2 or more.
All inputs are finite; a program needn't handle non-finite values.
Results may differ from a plain program's by a relative error of at most 0.006.
Values may be sent and summed in bfloat16 or wider, within the bound.
A program may use at most 128 MiB of HBM per device.

v0:
```python
import jax
import jax.numpy as jnp
from jax import lax
from jax.sharding import PartitionSpec as P


def shifted(value, axis, steps):
    count = lax.axis_size(axis)
    leading, last = (max(0, -steps), min(count, count - steps))
    return lax.ppermute(value, axis, [(source, source + steps) for source in range(leading, last)])


def body(
    features,
    cotangent,
    near_kernel,
    near_index,
    near_count,
    basis_in,
    basis_out,
    far_kernel,
    far_index,
    channel_mix,
):
    exact = lax.Precision.HIGHEST
    blocks, slots, panels, _ = near_kernel.shape
    width = features.shape[1]
    groups = lax.axis_size("curve")
    position = lax.axis_index("curve")
    chan_pos = lax.axis_index("chan")
    feat_blocks = features.reshape(blocks, panels, width)
    cot_blocks = cotangent.reshape(blocks, panels, width)
    live_slot = lax.iota(jnp.int32, slots)[None, :] < near_count[:, None]
    local_rows = near_index - (position * blocks - blocks)
    coarse = jnp.einsum(
        "brp,bpc->rc", basis_in, feat_blocks, preferred_element_type=jnp.float32
    ).astype(jnp.bfloat16)
    dfar = jnp.einsum("bpr,bpc->rc", basis_out, cot_blocks, preferred_element_type=jnp.float32)
    before = shifted(features, "curve", 1)
    extended = jnp.concatenate([before.reshape(blocks, panels, width), feat_blocks], axis=0)
    picked = extended[local_rows] * live_slot[:, :, None, None].astype(jnp.bfloat16)
    near = jnp.einsum("bspq,bsqc->bpc", near_kernel, picked, preferred_element_type=jnp.float32)
    mix_cols = lax.dynamic_slice_in_dim(channel_mix, chan_pos * width, width, 1)
    far_mats = far_kernel[0]
    partners = far_index[0]
    one_hot = (partners[:, None] == lax.iota(jnp.int32, groups)[None, :]).astype(jnp.float32)
    every = lax.all_gather(coarse[None], "curve", axis=0, tiled=True)
    chosen = jnp.einsum("ag,grc->arc", one_hot, every.astype(jnp.float32), precision=exact)
    partial_coef = jnp.einsum("aqr,arc->qc", far_mats, chosen, precision=exact)
    mix_rows = lax.dynamic_slice_in_dim(channel_mix, chan_pos * width, width, 0)
    term = jnp.dot(partial_coef, mix_rows, precision=exact, preferred_element_type=jnp.float32)
    far_coef = lax.psum_scatter(term, "chan", scatter_dimension=1, tiled=True)
    far_low = far_coef.astype(jnp.bfloat16)
    layer = near + jnp.einsum("bpr,rc->bpc", basis_out, far_low, preferred_element_type=jnp.float32)
    layer_out = layer.astype(jnp.bfloat16).reshape(blocks * panels, width)
    contrib = jnp.einsum(
        "bspq,bpc->bsqc", near_kernel, cot_blocks, preferred_element_type=jnp.float32
    )
    slot_hot = (
        (local_rows[:, :, None] == lax.iota(jnp.int32, 2 * blocks)[None, None, :])
        & live_slot[:, :, None]
    ).astype(jnp.bfloat16)
    contrib_high = contrib.astype(jnp.bfloat16)
    contrib_low = (contrib - contrib_high.astype(jnp.float32)).astype(jnp.bfloat16)
    spread_near = jnp.einsum(
        "bse,bsqc->eqc", slot_hot, contrib_high, preferred_element_type=jnp.float32
    )
    spread_near = spread_near + jnp.einsum(
        "bse,bsqc->eqc", slot_hot, contrib_low, preferred_element_type=jnp.float32
    )
    arrived = shifted(spread_near[:blocks].astype(jnp.bfloat16), "curve", -1).astype(jnp.float32)
    nearback = spread_near[blocks:] + arrived
    unmix_term = jnp.dot(dfar, mix_cols.T, precision=exact, preferred_element_type=jnp.float32)
    dz_share = lax.psum_scatter(unmix_term, "chan", scatter_dimension=1, tiled=True)
    spread = jnp.einsum("aqr,qc->arc", far_mats, dz_share, precision=exact)
    grad_terms = jnp.einsum("ag,arc->grc", one_hot, spread, precision=exact)
    dcoarse = lax.psum_scatter(grad_terms, "curve", scatter_dimension=0, tiled=True)[0]
    dcoarse_low = dcoarse.astype(jnp.bfloat16)
    grad = nearback + jnp.einsum(
        "brp,rc->bpc", basis_in, dcoarse_low, preferred_element_type=jnp.float32
    )
    feature_grad = grad.astype(jnp.bfloat16).reshape(blocks * panels, width)
    return (layer_out, feature_grad)


def solution(mesh):
    return jax.shard_map(
        body,
        mesh=mesh,
        in_specs=(
            P("curve", "chan"),
            P("curve", "chan"),
            P("curve", None, None, None),
            P("curve", None),
            P("curve"),
            P("curve", None, None),
            P("curve", None, None),
            P("curve", None, None, None),
            P("curve", None),
            P(),
        ),
        out_specs=(P("curve", "chan"), P("curve", "chan")),
        check_vma=False,
    )
```

profile of v0, /device:TPU:0, one launch (start us, length us, event | category | flops | bytes accessed | tf_op | source)
XLA Modules:
  0.0 174.2 jit_solution(17130858522322987509)
XLA Ops:
  7.2 0.7 iota_compare_fusion.2
  8.0 0.7 compare_select_fusion
  8.7 7.9 %subtract_convert_fusion = (bf16[32,8,128,128]{3,2,1,0:T(8,128)(2,1)}, bf16[32,8,128,128]{3,2,1,0:T(8,128)(2,1)S(1)}) fusion(bf16[32,8,128,128]{3,2,1,0:T(8,128)(2,1)} %param.12, bf16[32,128,128,1]{2,1,3,0:T(8,128)(2,1)S(1)} %bitcast.74), kind=kOutput, calls=%fused_computation.1 | convolution fusion | flops 1090519040 | bytes 26214400 | tf_op jit(solution)/shard_map/bspq,bpc->bsqc/dot_general | solution.py:56
  16.6 8.4 %fusion = f32[64,128,128,1]{2,0,3,1:T(8,128)S(1)} fusion(bf16[32,8,128,128]{3,2,1,0:T(8,128)(2,1)} %get-tuple-element.2, s32[32,8]{0,1:T(8,128)S(1)} %get-tuple-element.5, pred[32,8]{0,1:T(8,128)(4,1)S(1)} %get-tuple-element.6), kind=kOutput, calls=%fused_computation.2 | convolution fusion | flops 536903680 | bytes 12584192 | tf_op jit(solution)/shard_map/bse,bsqc->eqc/dot_general | solution.py:68
  25.1 5.5 %bitcast_add_fusion = f32[64,128,128]{2,0,1:T(8,128)S(1)} fusion(f32[64,128,128,1]{2,0,3,1:T(8,128)S(1)} %fusion, bf16[32,8,128,128]{3,2,1,0:T(8,128)(2,1)S(1)} %get-tuple-element.3, s32[32,8]{0,1:T(8,128)S(1)} %get-tuple-element.5, pred[32,8]{0,1:T(8,128)(4,1)S(1)} %get-tuple-element.6), kind=kOutput, calls=%fused_computation.8 | convolution fusion | flops 537952256 | bytes 16778496 | tf_op jit(solution)/shard_map/bse,bsqc->eqc/dot_general | solution.py:65
  30.6 1.9 %copy-done.1 = f32[64,128,128]{2,0,1:T(8,128)} copy-done((f32[64,128,128]{2,0,1:T(8,128)}, f32[64,128,128]{2,0,1:T(8,128)S(1)}, u32[]{:S(2)}) %copy-start.1) | copy-done | bytes 4194328
  32.5 1.2 slice.19
  33.8 1.3 collective-permute-start.1
  35.3 0.8 fusion.15
  36.2 4.0 %collective-permute-start = (bf16[4096,128]{1,0:T(8,128)(2,1)S(1)}, bf16[4096,128]{1,0:T(8,128)(2,1)}, u32[]{:S(2)}, u32[]{:S(2)}) collective-permute-start(bf16[4096,128]{1,0:T(8,128)(2,1)S(1)} %copy-done.2), channel_id=1, source_target_pairs={{0,2},{2,4},{4,6},{6,8},{8,10},{10,12},{12,14},{14,16},{16,18},{18... | collective-permute-start | bytes 3145736 | tf_op jit(solution)/shard_map/ppermute | solution.py:10
  40.6 32.8 %all-gather = bf16[256,128]{1,0:T(8,128)(2,1)S(1)} all-gather(bf16[16,128]{1,0:T(8,128)(2,1)S(1)} %fusion.14), channel_id=2, replica_groups=mesh['curve'=16,'chan'=2] {'curve'}, dimensions={0}, use_global_device_ids=true | all-gather | bytes 69632 | tf_op jit(solution)/shard_map/all_gather | solution.py:47
  73.8 0.8 fusion.17
  74.8 0.5 copy.33
  75.6 0.9 convolution_bitcast_fusion
  76.5 0.3 fusion.36
  76.8 0.7 copy.32
  77.5 7.1 %reduce-scatter.4.cloned.1.call-done = f32[16,128]{1,0:T(8,128)} async-done(((f32[16,256]{1,0:T(8,128)}), f32[16,128]{1,0:T(8,128)}) %reduce-scatter.4.cloned.1.call-update) | async-done | bytes 8208 | tf_op jit(solution)/shard_map/reduce_scatter | solution.py:52
  84.6 2.6 %fusion.31 = f32[128,32,128]{0,2,1:T(8,128)} fusion(bf16[32,128,16]{1,2,0:T(8,128)(2,1)S(1)} %copy-done.4, f32[16,128]{1,0:T(8,128)} %reduce-scatter.4.cloned.1.call-done), kind=kOutput, calls=%fused_computation.39 | convolution fusion | flops 16779264 | bytes 2236416 | tf_op jit(solution)/shard_map/bpr,rc->bpc/dot_general | solution.py:54
  87.2 56.6 %reduce-scatter.8.cloned.1.call-done = f32[1,16,128]{2,1,0:T(8,128)} async-done(((f32[16,16,128]{2,1,0:T(8,128)}), f32[1,16,128]{2,1,0:T(8,128)}) %reduce-scatter.8.cloned.1.call-update) | async-done | bytes 8208 | tf_op jit(solution)/shard_map/reduce_scatter | solution.py:77
  143.8 2.4 %fusion.10 = bf16[32,128,128]{2,0,1:T(8,128)(2,1)S(1)} fusion(f32[64,128,128]{2,0,1:T(8,128)} %copy-done.1, bf16[32,128,128]{2,0,1:T(8,128)(2,1)} %collective-permute-done.1, bf16[32,16,128]{0,1,2:T(8,128)(2,1)S(1)} %copy.33, f32[1,16,128]{2,1,0:T(8,128)} %reduce-scatter.8.cloned.1.call-done), kind=kOutput, calls=%fused_computation.13 | convolution fusion | flops 18876416 | bytes 4333568 | tf_op jit(solution)/shard_map/brp,rc->bpc/dot_general | solution.py:79
  146.2 1.4 copy.34
  147.6 1.7 pad_maximum_fusion
  149.3 8.5 %gather_fusion = bf16[256,128,128]{2,1,0:T(8,128)(2,1)} fusion(bf16[64,128,128]{2,1,0:T(8,128)(2,1)S(1)} %pad_maximum_fusion, s32[1024]{0:T(1024)S(1)} %pad_clamp_fusion), kind=kCustom, calls=%fused_computation | custom fusion | bytes 16778240 | tf_op jit(solution)/shard_map/gather | solution.py:41
  157.9 9.8 %fusion.11 = bf16[32,128,128]{2,1,0:T(8,128)(2,1)} fusion(f32[128,32,128]{0,2,1:T(8,128)} %fusion.31, bf16[32,8,128,128]{3,2,1,0:T(8,128)(2,1)} %param.12, bf16[32,8,128,128]{3,2,1,0:T(8,128)(2,1)} %bitcast.75, bf16[32,8]{1,0:T(8,128)(2,1)S(1)} %copy.25), kind=kOutput, calls=%fused_computation.16 | convolution fusion | flops 1091567616 | bytes 19923456 | tf_op jit(solution)/shard_map/bspq,bsqc->bpc/dot_general | solution.py:42
  (33 shorter events, 1.7 us)
Async XLA Ops:
  7.2 1.5 copy-start
  7.2 68.4 %reduce-scatter.6.cloned.1.call-start = ((), (), s32[]{:S(2)}) async-start(), calls=%async_computation.4 | async-start | bytes 24576 | tf_op jit(solution)/shard_map/reduce_scatter | solution.py:74
  25.0 10.0 %copy-start.4 = (bf16[32,128,16]{1,2,0:T(8,128)(2,1)S(1)}, bf16[32,128,16]{1,2,0:T(8,128)(2,1)}, u32[]{:S(2)}) copy-start(bf16[32,128,16]{1,2,0:T(8,128)(2,1)} %param.16) | copy-start | bytes 393220
  25.1 10.3 %copy-start.5 = (f32[256,256]{1,0:T(8,128)S(1)}, f32[256,256]{1,0:T(8,128)}, u32[]{:S(2)}) copy-start(f32[256,256]{1,0:T(8,128)} %param.19) | copy-start | bytes 786436
  25.1 11.2 %copy-start.2 = (bf16[4096,128]{1,0:T(8,128)(2,1)S(1)}, bf16[4096,128]{1,0:T(8,128)(2,1)}, u32[]{:S(2)}) copy-start(bf16[4096,128]{1,0:T(8,128)(2,1)} %param.10) | copy-start | bytes 3145732
  25.1 15.2 %copy-start.6 = (f32[1,8,16,16]{3,2,1,0:T(8,128)S(1)}, f32[1,8,16,16]{3,2,1,0:T(8,128)}, u32[]{:S(2)}) copy-start(f32[1,8,16,16]{3,2,1,0:T(8,128)} %param.17) | copy-start | bytes 24580
  25.1 15.2 %copy-start.3 = (bf16[32,16,128]{2,1,0:T(8,128)(2,1)S(1)}, bf16[32,16,128]{2,1,0:T(8,128)(2,1)}, u32[]{:S(2)}) copy-start(bf16[32,16,128]{2,1,0:T(8,128)(2,1)} %param.15) | copy-start | bytes 393220
  25.1 48.2 %copy-start.7 = (s32[1,8]{1,0:T(1,128)S(1)}, s32[1,8]{1,0:T(1,128)}, u32[]{:S(2)}) copy-start(s32[1,8]{1,0:T(1,128)} %param.18) | copy-start | bytes 100
  30.6 2.0 %copy-start.1 = (f32[64,128,128]{2,0,1:T(8,128)}, f32[64,128,128]{2,0,1:T(8,128)S(1)}, u32[]{:S(2)}) copy-start(f32[64,128,128]{2,0,1:T(8,128)S(1)} %bitcast_add_fusion) | copy-start | bytes 12582916
  33.8 110.0 %collective-permute-start.1 = (bf16[32,128,128]{2,0,1:T(8,128)(2,1)}, bf16[32,128,128]{2,0,1:T(8,128)(2,1)}, u32[]{:S(2)}, u32[]{:S(2)}) collective-permute-start(bf16[32,128,128]{2,0,1:T(8,128)(2,1)} %slice.19), channel_id=1, source_target_pairs={{2,0},{4,2},{6,4},{8,6},{10,8},{12,10},{14,12},{16,14},{18,16},{20... | collective-permute-start | bytes 3145736 | tf_op jit(solution)/shard_map/ppermute | solution.py:10
  36.2 48.4 %reduce-scatter.4.cloned.1.call-start = ((), (), s32[]{:S(2)}) async-start(), calls=%async_computation.3 | async-start | bytes 24576 | tf_op jit(solution)/shard_map/reduce_scatter | solution.py:52
  36.2 111.4 %collective-permute-start = (bf16[4096,128]{1,0:T(8,128)(2,1)S(1)}, bf16[4096,128]{1,0:T(8,128)(2,1)}, u32[]{:S(2)}, u32[]{:S(2)}) collective-permute-start(bf16[4096,128]{1,0:T(8,128)(2,1)S(1)} %copy-done.2), channel_id=1, source_target_pairs={{0,2},{2,4},{4,6},{6,8},{8,10},{10,12},{12,14},{14,16},{16,18},{18... | collective-permute-start | bytes 3145736 | tf_op jit(solution)/shard_map/ppermute | solution.py:10
  74.6 69.2 %reduce-scatter.8.cloned.1.call-start = ((), (), s32[]{:S(2)}) async-start(), calls=%async_computation.5 | async-start | bytes 139264 | tf_op jit(solution)/shard_map/reduce_scatter | solution.py:77
Sparse Core Ops, SparseCore 0:
  36.3 14.2 reduce-scatter.5
  74.7 9.8 reduce-scatter.3
  88.7 55.0 reduce-scatter.7
where the time goes:
time: 175 us; the launch traced here: 174 us
  waiting for transfers between devices  63.7 us (36%)
  matrix products  40.4 us (23%)
  blocking collectives  32.8 us (19%)
  local copies, waits for them, and re-layouts  14.6 us (8%)
  between operations  13.9 us (8%)
  starting transfers between devices  5.58 us (3%)
  other arithmetic  3.16 us (2%)
    reduce_scatter x1, waiting for transfers between devices, body(): lax.psum_scatter(grad_terms, 'curve', scatter_dimension=0, tiled=True)[0]  56.6 us
    all_gather x1, blocking collectives, body(): every = lax.all_gather(coarse[None], 'curve', axis=0, tiled=True)  32.8 us
    dot_general x1, matrix products, body(): jnp.einsum('bspq,bsqc->bpc', near_kernel, picked, preferred_element_type=...  9.79 us
    gather x1, local copies, waits for them, and re-layouts, body(): extended[local_rows] * live_slot[:, :, None, None].astype(jnp.bfloat16)  8.54 us
    dot_general x1, matrix products, body(): jnp.einsum('bse,bsqc->eqc', slot_hot, contrib_low, preferred_element_type...  8.44 us
    dot_general x1, matrix products, body(): jnp.einsum('bspq,bpc->bsqc', near_kernel, cot_blocks, preferred_element_t...  7.93 us
    reduce_scatter x1, waiting for transfers between devices, body(): far_coef = lax.psum_scatter(term, 'chan', scatter_dimension=1, tiled=True)  7.07 us
    dot_general x1, matrix products, body(): jnp.einsum('bse,bsqc->eqc', slot_hot, contrib_high, preferred_element_typ...  5.47 us
  transfers between devices with their start and end apart: 5, of which 2 were waited for; matrix products, arithmetic and copies ran while one was open for 7% of the time, Pallas kernels for 0%

commit v1 on v0

v1 whole, which is shorter than its diff:
```python
import functools

import jax
import jax.numpy as jnp
from jax import lax
from jax.experimental import pallas as pl
from jax.experimental.pallas import tpu as pltpu
from jax.sharding import PartitionSpec as P

F32 = jnp.float32
BF16 = jnp.bfloat16
EXACT = lax.Precision.HIGHEST
VMEM_LIMIT = 40 * 1024 * 1024
STEP = 4


def shifted(value, axis, steps):
    count = lax.axis_size(axis)
    leading, last = (max(0, -steps), min(count, count - steps))
    return lax.ppermute(value, axis, [(source, source + steps) for source in range(leading, last)])


def cover(shape):
    zeros = (0,) * len(shape)
    return pl.BlockSpec(shape, lambda *_: zeros)


def params():
    return pltpu.CompilerParams(vmem_limit_bytes=VMEM_LIMIT)


def bundle_kernel(chan_ref, x_ref, dy_ref, bin_ref, bout_ref, far_ref, part_ref, out_ref):
    blocks, rank, width = bin_ref.shape[0], bin_ref.shape[1], x_ref.shape[2]
    coarse = jnp.zeros((rank, width), F32)
    dfar = jnp.zeros((rank, width), F32)
    for b in range(blocks):
        coarse += jnp.dot(bin_ref[b], x_ref[b], preferred_element_type=F32)
        dfar += lax.dot_general(
            bout_ref[b], dy_ref[b], (((0,), (0,)), ((), ())), preferred_element_type=F32
        )
    out_ref[0:rank] = coarse.astype(BF16)
    out_ref[rank : 2 * rank] = dfar.astype(BF16)
    far = far_ref[...]
    high = far.astype(BF16).astype(F32)
    low = far - high
    out_ref[2 * rank : 3 * rank] = jnp.where(chan_ref[0] == 0, high, low).astype(BF16)
    out_ref[3 * rank : 4 * rank] = jnp.broadcast_to(part_ref[...], (rank, width)).astype(BF16)


def far_kernel_body(rank, place_ref, part_ref, every_ref, far_ref, mix_ref, far_out, back_out):
    group, chan = place_ref[0], place_ref[1]
    shares = mix_ref.shape[0] // far_out.shape[1]
    width = far_out.shape[1]
    groups = every_ref.shape[0] // shares
    partners = far_ref.shape[1] // rank
    cols = pl.ds(pl.multiple_of(chan * width, width), width)
    far = far_ref[...]
    high = far.astype(BF16)
    low = (far - high.astype(F32)).astype(BF16)
    picked = jnp.concatenate(
        [
            jnp.concatenate(
                [every_ref[part_ref[a] * shares + s, 0:rank] for a in range(partners)], axis=0
            )
            for s in range(shares)
        ],
        axis=1,
    )
    coef = jnp.dot(high, picked, preferred_element_type=F32) + jnp.dot(
        low, picked, preferred_element_type=F32
    )
    far_out[...] = jnp.dot(
        coef, mix_ref[:, cols], precision=EXACT, preferred_element_type=F32
    ).astype(BF16)
    total = jnp.zeros((partners * rank, shares * width), F32)
    span = min(groups, 16)
    for first in range(0, groups, span):
        grads = jnp.concatenate(
            [
                jnp.concatenate(
                    [
                        every_ref[g * shares + s, rank : 2 * rank]
                        for g in range(first, first + span)
                    ],
                    axis=0,
                )
                for s in range(shares)
            ],
            axis=1,
        )
        for s in range(2):
            mats = []
            for g in range(first, first + span):
                here = every_ref[g * shares + s, 3 * rank : 4 * rank].astype(F32) == group.astype(F32)
                mats.append(
                    jnp.where(here, every_ref[g * shares + s, 2 * rank : 3 * rank].astype(F32), 0.0)
                )
            chosen = jnp.concatenate(mats, axis=0).astype(BF16)
            total += lax.dot_general(
                chosen, grads, (((0,), (0,)), ((), ())), preferred_element_type=F32
            )
    dmixed = total[0:rank]
    for a in range(1, partners):
        dmixed += total[a * rank : (a + 1) * rank]
    back_out[...] = lax.dot_general(
        dmixed,
        mix_ref[cols, :],
        (((1,), (1,)), ((), ())),
        precision=EXACT,
        preferred_element_type=F32,
    ).astype(BF16)


def backward_kernel(target_ref, tile_ref, dy_ref, left_ref, own_ref, total):
    step = pl.program_id(0)
    blocks = left_ref.shape[0]
    slots, panels = tile_ref.shape[1], tile_ref.shape[2]

    @pl.when(step == 0)
    def _():
        @pl.loop(0, 2 * blocks)
        def _(row):
            total[row] = jnp.zeros(total.shape[1:], F32)

    for i in range(STEP):
        turned = dy_ref[i].T
        first = (step * STEP + i) * slots
        for k in range(0, slots, 2):
            pair = jnp.concatenate([tile_ref[i, k], tile_ref[i, k + 1]], axis=1)
            term = jnp.dot(turned, pair, preferred_element_type=F32)
            total[target_ref[first + k]] += term[:, :panels]
            total[target_ref[first + k + 1]] += term[:, panels:]

    @pl.when(step == pl.num_programs(0) - 1)
    def _():
        @pl.loop(0, blocks)
        def _(row):
            left_ref[row] = total[row].astype(BF16)
            own_ref[row] = total[blocks + row]


def forward_kernel(source_ref, tile_ref, before_ref, x_ref, bout_ref, far_ref, out_ref, held):
    step = pl.program_id(0)
    blocks = x_ref.shape[0]
    slots = tile_ref.shape[1]

    @pl.when(step == 0)
    def _():
        @pl.loop(0, blocks)
        def _(row):
            held[row] = before_ref[row]
            held[blocks + row] = x_ref[row]

        held[2 * blocks] = jnp.zeros(held.shape[1:], BF16)

    far = far_ref[...]
    for i in range(STEP):
        first = (step * STEP + i) * slots
        tiles = jnp.concatenate([tile_ref[i, k] for k in range(slots)], axis=1)
        rows = jnp.concatenate([held[source_ref[first + k]] for k in range(slots)], axis=0)
        near = jnp.dot(tiles, rows, preferred_element_type=F32)
        near += jnp.dot(bout_ref[i], far, preferred_element_type=F32)
        out_ref[i] = near.astype(BF16)


def gradient_kernel(own_ref, arrived_ref, bin_ref, back_ref, out_ref):
    back = back_ref[...]
    for i in range(own_ref.shape[0]):
        turned = own_ref[i] + arrived_ref[i].astype(F32)
        term = lax.dot_general(
            back, bin_ref[i], (((0,), (0,)), ((), ())), preferred_element_type=F32
        )
        out_ref[i] = (turned + term).T.astype(BF16)


def body(
    features,
    cotangent,
    near_kernel,
    near_index,
    near_count,
    basis_in,
    basis_out,
    far_kernel,
    far_index,
    channel_mix,
):
    blocks, slots, panels, _ = near_kernel.shape
    width = features.shape[1]
    rank = basis_in.shape[1]
    partners = far_index.shape[1]
    position = lax.axis_index("curve")
    chan_pos = lax.axis_index("chan")
    x = features.reshape(blocks, panels, width)
    dy = cotangent.reshape(blocks, panels, width)
    before = shifted(features, "curve", 1).reshape(blocks, panels, width)
    live_slot = lax.iota(jnp.int32, slots)[None, :] < near_count[:, None]
    rows = near_index - (position * blocks - blocks)
    rows = jnp.where(live_slot, rows, 2 * blocks).reshape(-1)
    far_flat = far_kernel[0].transpose(1, 0, 2).reshape(rank, partners * rank)
    part_row = jnp.repeat(far_index[0], rank)[None, :].astype(F32)
    tile_shape = (panels, width)
    steps = (blocks // STEP,)

    def by_step(*shape):
        zeros = (0,) * (len(shape) - 1)
        return pl.BlockSpec(shape, lambda n, *_: (n,) + zeros)

    own_bundle = pl.pallas_call(
        bundle_kernel,
        out_shape=jax.ShapeDtypeStruct((4 * rank, width), BF16),
        in_specs=[pl.BlockSpec(memory_space=pltpu.SMEM)]
        + [pl.BlockSpec(memory_space=pltpu.VMEM)] * 6,
        out_specs=pl.BlockSpec(memory_space=pltpu.VMEM),
        compiler_params=params(),
        name="bundle",
    )(chan_pos[None], x, dy, basis_in, basis_out, far_flat, part_row)
    every = lax.all_gather(own_bundle, ("curve", "chan"), axis=0)

    half_flops = 2 * blocks * slots * panels * panels * width
    tile_bytes = 2 * near_kernel.size
    left, own = pl.pallas_call(
        backward_kernel,
        out_shape=(
            jax.ShapeDtypeStruct((blocks, width, panels), BF16),
            jax.ShapeDtypeStruct((blocks, width, panels), F32),
        ),
        grid_spec=pltpu.PrefetchScalarGridSpec(
            num_scalar_prefetch=1,
            grid=steps,
            in_specs=[by_step(STEP, slots, panels, panels), by_step(STEP, *tile_shape)],
            out_specs=(cover((blocks, width, panels)), cover((blocks, width, panels))),
            scratch_shapes=[pltpu.VMEM((2 * blocks + 1, width, panels), F32)],
        ),
        compiler_params=params(),
        cost_estimate=pl.CostEstimate(
            flops=4 * half_flops, bytes_accessed=2 * tile_bytes, transcendentals=0
        ),
        name="backward",
    )(rows, near_kernel, dy)
    arrived = shifted(left, "curve", -1)

    place = jnp.stack([position, chan_pos]).astype(jnp.int32)
    far_low, back_low = pl.pallas_call(
        functools.partial(far_kernel_body, rank),
        out_shape=(
            jax.ShapeDtypeStruct((rank, width), BF16),
            jax.ShapeDtypeStruct((rank, width), BF16),
        ),
        in_specs=[pl.BlockSpec(memory_space=pltpu.SMEM)] * 2
        + [pl.BlockSpec(memory_space=pltpu.VMEM)] * 3,
        out_specs=(pl.BlockSpec(memory_space=pltpu.VMEM),) * 2,
        compiler_params=params(),
        name="far",
    )(place, far_index[0], every, far_flat, channel_mix)

    layer = pl.pallas_call(
        forward_kernel,
        out_shape=jax.ShapeDtypeStruct((blocks, panels, width), BF16),
        grid_spec=pltpu.PrefetchScalarGridSpec(
            num_scalar_prefetch=1,
            grid=steps,
            in_specs=[
                by_step(STEP, slots, panels, panels),
                cover((blocks, panels, width)),
                cover((blocks, panels, width)),
                by_step(STEP, panels, rank),
                cover((rank, width)),
            ],
            out_specs=by_step(STEP, *tile_shape),
            scratch_shapes=[pltpu.VMEM((2 * blocks + 1, panels, width), BF16)],
        ),
        compiler_params=params(),
        cost_estimate=pl.CostEstimate(
            flops=4 * half_flops, bytes_accessed=2 * tile_bytes, transcendentals=0
        ),
        name="forward",
    )(rows, near_kernel, before, x, basis_out, far_low)

    grad = pl.pallas_call(
        gradient_kernel,
        out_shape=jax.ShapeDtypeStruct((blocks, panels, width), BF16),
        grid=steps,
        in_specs=[
            by_step(STEP, width, panels),
            by_step(STEP, width, panels),
            by_step(STEP, rank, panels),
            cover((rank, width)),
        ],
        out_specs=by_step(STEP, *tile_shape),
        compiler_params=params(),
        name="gradient",
    )(own, arrived, basis_in, back_low)
    return (layer.reshape(blocks * panels, width), grad.reshape(blocks * panels, width))


def solution(mesh):
    return jax.shard_map(
        body,
        mesh=mesh,
        in_specs=(
            P("curve", "chan"),
            P("curve", "chan"),
            P("curve", None, None, None),
            P("curve", None),
            P("curve"),
            P("curve", None, None),
            P("curve", None, None),
            P("curve", None, None, None),
            P("curve", None),
            P(),
        ),
        out_specs=(P("curve", "chan"), P("curve", "chan")),
        check_vma=False,
    )
```

time: 175 us -> 116 us (0.66)
  waiting for transfers between devices: 63.7 us -> 0.01 us
  blocking collectives: 32.8 us -> 73.7 us
  matrix products: 40.4 us -> 0 us
  Pallas kernels: 0 us -> 21.4 us
  between operations: 13.9 us -> 0.78 us
  other arithmetic: 3.16 us -> 0.77 us
    reduce_scatter x3 -> x0, waiting for transfers between devices: 63.7 us -> none  [the longest x1 56.6 us: body(): lax.psum_scatter(grad_terms, 'curve', scatter_dimension=0, tiled=True)[0]]
    all_gather x1, blocking collectives: 32.8 us -> 73.7 us  [body(): every = lax.all_gather(own_bundle, ('curve', 'chan'), axis=0)]
    dot_general x14 -> x0, matrix products: 40.4 us -> none  [the longest x1 9.79 us: body(): jnp.einsum('bspq,bsqc->bpc', near_kernel, picked, preferred_element_type=...]
    pallas_call x0 -> x5, Pallas kernels: none -> 21.4 us  [the longest x1 6.96 us: body(): pl.pallas_call(forward_kernel, out_shape=jax.ShapeDtypeStruct((blocks, pa...]
    unnamed x17 -> x23, local copies, waits for them, and re-layouts: 2.46 us -> 13.7 us
    gather x1 -> x0, local copies, waits for them, and re-layouts: 8.54 us -> none  [body(): extended[local_rows] * live_slot[:, :, None, None].astype(jnp.bfloat16)]
  transfers between devices with their start and end apart: 5 -> 2, of which waited for: 2 -> 0; matrix products, arithmetic and copies ran while one was open for 7% -> 2% of each run, Pallas kernels for 0% -> 13%
where the time goes in v1:
time: 116 us; the launch traced here: 115 us
  blocking collectives  73.7 us (64%)
  Pallas kernels  21.4 us (18%)
  local copies, waits for them, and re-layouts  14.1 us (12%)
  starting transfers between devices  4.63 us (4%)
    all_gather x1, blocking collectives, body(): every = lax.all_gather(own_bundle, ('curve', 'chan'), axis=0)  73.7 us
    unnamed x23, local copies, waits for them, and re-layouts  13.7 us
    pallas_call x1, Pallas kernels, body(): pl.pallas_call(forward_kernel, out_shape=jax.ShapeDtypeStruct((blocks, pa...  6.96 us
    pallas_call x1, Pallas kernels, body(): pl.pallas_call(backward_kernel, out_shape=(jax.ShapeDtypeStruct((blocks,...  6.38 us
    pallas_call x1, Pallas kernels, body(): pl.pallas_call(gradient_kernel, out_shape=jax.ShapeDtypeStruct((blocks, p...  6.3 us
    ppermute x2, starting transfers between devices, shifted(): lax.ppermute(value, axis, [(source, source + steps) for source in range(l...  4.63 us
  transfers between devices with their start and end apart: 2, of which 0 were waited for; matrix products, arithmetic and copies ran while one was open for 2% of the time, Pallas kernels for 13%

profile of v1, /device:TPU:0, one launch (start us, length us, event | category | flops | bytes accessed | tf_op | source)
XLA Modules:
  0.0 115.5 jit_solution(10288203773274696695)
XLA Ops:
  0.6 3.4 %collective-permute-start = (bf16[4096,128]{1,0:T(8,128)(2,1)}, bf16[4096,128]{1,0:T(8,128)(2,1)}, u32[]{:S(2)}, u32[]{:S(2)}) collective-permute-start(bf16[4096,128]{1,0:T(8,128)(2,1)} %param.10), channel_id=1, source_target_pairs={{0,2},{2,4},{4,6},{6,8},{8,10},{10,12},{12,14},{14,16},{16,18},{18... | collective-permute-start | bytes 3145736 | tf_op jit(solution)/shard_map/ppermute | solution.py:20
  4.0 0.7 subtract_select_fusion
  4.7 0.1 copy.15
  4.8 0.1 reshape.39.source_ref.target_ref
  4.9 1.2 %copy-done = bf16[4096,128]{1,0:T(8,128)(2,1)S(1)} copy-done((bf16[4096,128]{1,0:T(8,128)(2,1)S(1)}, bf16[4096,128]{1,0:T(8,128)(2,1)}, u32[]{:S(2)}) %copy-start) | copy-done | bytes 1048600
  6.1 3.4 %copy-done.8 = bf16[32,8,128,128]{3,2,1,0:T(8,128)(2,1)S(1)} copy-done((bf16[32,8,128,128]{3,2,1,0:T(8,128)(2,1)S(1)}, bf16[32,8,128,128]{3,2,1,0:T(8,128)(2,1)}, u32[]{:S(2)}) %copy-start.8) | copy-done | bytes 8388632
  9.5 6.4 %backward.1 = (bf16[32,128,128]{2,1,0:T(8,128)(2,1)}, f32[32,128,128]{2,1,0:T(8,128)S(1)}) custom-call(s32[256]{0:T(256)S(1)} %reshape.39.source_ref.target_ref, bf16[32,8,128,128]{3,2,1,0:T(8,128)(2,1)S(1)} %copy-done.8, bf16[32,128,128]{2,1,0:T(8,128)(2,1)S(1)} %bitcast.14), custom_call_target="tpu_custom_call" | custom-call | flops 4294967296 | bytes 16777216 | tf_op jit(solution)/shard_map/backward/pallas_call | solution.py:222
  15.8 1.3 %collective-permute-start.1 = (bf16[32,128,128]{2,1,0:T(8,128)(2,1)}, bf16[32,128,128]{2,1,0:T(8,128)(2,1)}, u32[]{:S(2)}, u32[]{:S(2)}) collective-permute-start(bf16[32,128,128]{2,1,0:T(8,128)(2,1)} %get-tuple-element.8), channel_id=1, source_target_pairs={{2,0},{4,2},{6,4},{8,6},{10,8},{12,10},{14,12},{16,14},{18,16},{20... | collective-permute-start | bytes 3145736 | tf_op jit(solution)/shard_map/ppermute | solution.py:20
  17.2 0.1 broadcast_in_dim.11
  17.2 0.1 convert_element_type.6.part_ref
  17.3 0.1 reshape.43.far_ref
  17.4 1.4 %copy.18.bout_ref = bf16[32,128,16]{2,1,0:T(8,128)(2,1)S(1)} copy(bf16[32,128,16]{1,2,0:T(8,128)(2,1)} %param.16) | data formatting | bytes 262144 | tf_op args[6]
  18.8 1.2 %copy-done.1 = bf16[4096,128]{1,0:T(8,128)(2,1)S(1)} copy-done((bf16[4096,128]{1,0:T(8,128)(2,1)S(1)}, bf16[4096,128]{1,0:T(8,128)(2,1)}, u32[]{:S(2)}) %copy-start.1) | copy-done | bytes 1048600
  20.1 1.2 %copy-done.2 = bf16[4096,128]{1,0:T(8,128)(2,1)S(1)} copy-done((bf16[4096,128]{1,0:T(8,128)(2,1)S(1)}, bf16[4096,128]{1,0:T(8,128)(2,1)}, u32[]{:S(2)}) %copy-start.2) | copy-done | bytes 1048600
  21.3 0.7 bundle.1
  22.0 0.1 pad_add_fusion.place_ref
  22.0 73.7 %all-gather = bf16[2048,128]{1,0:T(8,128)(2,1)S(1)} all-gather(bf16[64,128]{1,0:T(8,128)(2,1)S(1)} %bundle.1), channel_id=2, replica_groups=mesh['curve'=16,'chan'=2] {'curve','chan'}, dimensions={0}, use_global_device_ids=true | all-gather | bytes 540672 | tf_op jit(solution)/shard_map/all_gather | solution.py:218
  95.8 0.7 copy-done.7
  96.4 1.1 far.1
  97.5 0.0 copy-start.3
  97.6 1.2 %copy-done.3 = bf16[4096,128]{1,0:T(8,128)(2,1)S(1)} copy-done((bf16[4096,128]{1,0:T(8,128)(2,1)S(1)}, bf16[4096,128]{1,0:T(8,128)(2,1)}, u32[]{:S(2)}) %copy-start.3) | copy-done | bytes 1048600
  98.8 3.4 %copy-done.9 = bf16[32,8,128,128]{3,2,1,0:T(8,128)(2,1)S(1)} copy-done((bf16[32,8,128,128]{3,2,1,0:T(8,128)(2,1)S(1)}, bf16[32,8,128,128]{3,2,1,0:T(8,128)(2,1)}, u32[]{:S(2)}) %copy-start.9) | copy-done | bytes 8388632
  102.2 7.0 %forward.1 = bf16[32,128,128]{2,1,0:T(8,128)(2,1)} custom-call(s32[256]{0:T(256)S(1)} %reshape.39.source_ref.target_ref, bf16[32,8,128,128]{3,2,1,0:T(8,128)(2,1)S(1)} %copy-done.9, bf16[32,128,128]{2,1,0:T(8,128)(2,1)} %bitcast.before_ref, bf16[32,128,128]{2,1,0:T(8,128)(2,1)S(1)} %bitcast.17, bf16[32,128,16]{2,1,0:T(8,128)(2,1)S(1)} %copy.18.bout_ref, ...), custom_call_target="tpu_custom_call" | custom-call | flops 4294967296 | bytes 16777216 | tf_op jit(solution)/shard_map/forward/pallas_call | solution.py:257
  109.2 6.3 %gradient.1 = bf16[32,128,128]{2,1,0:T(8,128)(2,1)} custom-call(f32[32,128,128]{2,1,0:T(8,128)S(1)} %get-tuple-element.7.own_ref, bf16[32,128,128]{2,1,0:T(8,128)(2,1)} %collective-permute-done.1.arrived_ref, bf16[32,16,128]{2,1,0:T(8,128)(2,1)S(1)} %copy-done.4, bf16[16,128]{1,0:T(8,128)(2,1)S(1)} %get-tuple-element.9.back_ref), custom_call_target="tpu_custom_call" | custom-call | tf_op jit(solution)/shard_map/gradient/pallas_call | solution.py:280
  (18 shorter events, 0.1 us)
Async XLA Ops:
  0.6 16.5 %copy-start.6 = (s32[1,8]{1,0:T(1,128)S(1)}, s32[1,8]{1,0:T(1,128)}, u32[]{:S(2)}) copy-start(s32[1,8]{1,0:T(1,128)} %param.18) | copy-start | bytes 100
  0.6 96.9 %collective-permute-start = (bf16[4096,128]{1,0:T(8,128)(2,1)}, bf16[4096,128]{1,0:T(8,128)(2,1)}, u32[]{:S(2)}, u32[]{:S(2)}) collective-permute-start(bf16[4096,128]{1,0:T(8,128)(2,1)} %param.10), channel_id=1, source_target_pairs={{0,2},{2,4},{4,6},{6,8},{8,10},{10,12},{12,14},{14,16},{16,18},{18... | collective-permute-start | bytes 3145736 | tf_op jit(solution)/shard_map/ppermute | solution.py:20
  4.9 1.2 %copy-start = (bf16[4096,128]{1,0:T(8,128)(2,1)S(1)}, bf16[4096,128]{1,0:T(8,128)(2,1)}, u32[]{:S(2)}) copy-start(bf16[4096,128]{1,0:T(8,128)(2,1)} %param.11) | copy-start | bytes 3145732
  6.1 3.4 %copy-start.8 = (bf16[32,8,128,128]{3,2,1,0:T(8,128)(2,1)S(1)}, bf16[32,8,128,128]{3,2,1,0:T(8,128)(2,1)}, u32[]{:S(2)}) copy-start(bf16[32,8,128,128]{3,2,1,0:T(8,128)(2,1)} %tile_ref.3) | copy-start | bytes 25165828
  9.5 7.8 %copy-start.10 = (f32[1,8,16,16]{3,2,1,0:T(8,128)S(1)}, f32[1,8,16,16]{3,2,1,0:T(8,128)}, u32[]{:S(2)}) copy-start(f32[1,8,16,16]{3,2,1,0:T(8,128)} %param.17) | copy-start | bytes 24580
  9.5 9.3 %copy-start.4 = (bf16[32,16,128]{2,1,0:T(8,128)(2,1)S(1)}, bf16[32,16,128]{2,1,0:T(8,128)(2,1)}, u32[]{:S(2)}) copy-start(bf16[32,16,128]{2,1,0:T(8,128)(2,1)} %bin_ref.3) | copy-start | bytes 393220
  9.5 86.3 %copy-start.5 = (f32[256,256]{1,0:T(8,128)S(1)}, f32[256,256]{1,0:T(8,128)}, u32[]{:S(2)}) copy-start(f32[256,256]{1,0:T(8,128)} %mix_ref.1) | copy-start | bytes 786436
  15.8 93.3 %collective-permute-start.1 = (bf16[32,128,128]{2,1,0:T(8,128)(2,1)}, bf16[32,128,128]{2,1,0:T(8,128)(2,1)}, u32[]{:S(2)}, u32[]{:S(2)}) collective-permute-start(bf16[32,128,128]{2,1,0:T(8,128)(2,1)} %get-tuple-element.8), channel_id=1, source_target_pairs={{2,0},{4,2},{6,4},{8,6},{10,8},{12,10},{14,12},{16,14},{18,16},{20... | collective-permute-start | bytes 3145736 | tf_op jit(solution)/shard_map/ppermute | solution.py:20
  18.8 1.2 %copy-start.1 = (bf16[4096,128]{1,0:T(8,128)(2,1)S(1)}, bf16[4096,128]{1,0:T(8,128)(2,1)}, u32[]{:S(2)}) copy-start(bf16[4096,128]{1,0:T(8,128)(2,1)} %param.11) | copy-start | bytes 3145732
  20.0 1.2 %copy-start.2 = (bf16[4096,128]{1,0:T(8,128)(2,1)S(1)}, bf16[4096,128]{1,0:T(8,128)(2,1)}, u32[]{:S(2)}) copy-start(bf16[4096,128]{1,0:T(8,128)(2,1)} %param.10) | copy-start | bytes 3145732
  95.8 0.7 copy-start.7
  97.5 1.3 %copy-start.3 = (bf16[4096,128]{1,0:T(8,128)(2,1)S(1)}, bf16[4096,128]{1,0:T(8,128)(2,1)}, u32[]{:S(2)}) copy-start(bf16[4096,128]{1,0:T(8,128)(2,1)} %param.10) | copy-start | bytes 3145732
  98.8 3.4 %copy-start.9 = (bf16[32,8,128,128]{3,2,1,0:T(8,128)(2,1)S(1)}, bf16[32,8,128,128]{3,2,1,0:T(8,128)(2,1)}, u32[]{:S(2)}) copy-start(bf16[32,8,128,128]{3,2,1,0:T(8,128)(2,1)} %tile_ref.3) | copy-start | bytes 25165828

commit v2 on v1

v2 whole, which is shorter than its diff:
```python
import functools

import jax
import jax.numpy as jnp
from jax import lax
from jax.experimental import pallas as pl
from jax.experimental.pallas import tpu as pltpu
from jax.sharding import PartitionSpec as P

F32 = jnp.float32
BF16 = jnp.bfloat16
EXACT = lax.Precision.HIGHEST
VMEM_LIMIT = 60 * 1024 * 1024
STEP = 4


def shifted(value, axis, steps):
    count = lax.axis_size(axis)
    leading, last = (max(0, -steps), min(count, count - steps))
    return lax.ppermute(value, axis, [(source, source + steps) for source in range(leading, last)])


def cover(shape):
    zeros = (0,) * len(shape)
    return pl.BlockSpec(shape, lambda *_: zeros)


def params(mib=60):
    return pltpu.CompilerParams(vmem_limit_bytes=mib * 1024 * 1024)


def bundle_kernel(part_ref, x_ref, dy_ref, bin_ref, bout_ref, far_ref, out_ref):
    blocks, rank, width = bin_ref.shape[0], bin_ref.shape[1], x_ref.shape[2]
    partners = far_ref.shape[0]
    coarse = jnp.zeros((rank, width), F32)
    dfar = jnp.zeros((rank, width), F32)
    for b in range(blocks):
        coarse += jnp.dot(bin_ref[b], x_ref[b], preferred_element_type=F32)
        dfar += lax.dot_general(
            bout_ref[b], dy_ref[b], (((0,), (0,)), ((), ())), preferred_element_type=F32
        )
    coarse = coarse.astype(BF16)
    spread = [
        lax.dot_general(
            far_ref[a], dfar, (((0,), (0,)), ((), ())), precision=EXACT, preferred_element_type=F32
        )
        for a in range(partners)
    ]

    @pl.loop(0, out_ref.shape[0])
    def _(group):
        share = jnp.zeros((rank, width), F32)
        for a in range(partners):
            share += jnp.where(part_ref[a] == group, 1.0, 0.0) * spread[a]
        out_ref[group, 0:rank] = coarse
        out_ref[group, rank : 2 * rank] = share.astype(BF16)


def exchange_kernel(
    groups, shares, part_ref, send_ref, far_ref, mix_ref, far_out, back_out,
    held, halves, joined, send_sem, recv_sem, send_half, recv_half,
):
    me, chan = lax.axis_index("curve"), lax.axis_index("chan")
    rank, width = far_out.shape
    partners = far_ref.shape[0]
    barrier = pltpu.get_barrier_semaphore()

    @pl.loop(1, groups)
    def _(step):
        pl.semaphore_signal(
            barrier,
            inc=1,
            device_id=(lax.rem(me + step, groups), chan),
            device_id_type=pl.DeviceIdType.MESH,
        )

    for step in range(1, shares):
        pl.semaphore_signal(
            barrier,
            inc=1,
            device_id=(me, lax.rem(chan + step, shares)),
            device_id_type=pl.DeviceIdType.MESH,
        )
    pl.semaphore_wait(barrier, groups + shares - 2)

    def along_curve(step):
        other = lax.rem(me + step, groups)
        return pltpu.make_async_remote_copy(
            src_ref=send_ref.at[other],
            dst_ref=held.at[me],
            send_sem=send_sem.at[step],
            recv_sem=recv_sem.at[step],
            device_id=(other, chan),
            device_id_type=pl.DeviceIdType.MESH,
        )

    @pl.loop(1, groups)
    def _(step):
        along_curve(step).start()

    held[me] = send_ref[me]

    @pl.loop(1, groups)
    def _(step):
        along_curve(step).wait()

    coef = jnp.zeros((rank, width), F32)
    for a in range(partners):
        far = far_ref[a]
        high = far.astype(BF16)
        low = (far - high.astype(F32)).astype(BF16)
        row = held[part_ref[a], 0:rank]
        coef += jnp.dot(high, row, preferred_element_type=F32)
        coef += jnp.dot(low, row, preferred_element_type=F32)
    total = lax.fori_loop(
        0,
        groups,
        lambda g, acc: acc + held[g, rank : 2 * rank].astype(F32),
        jnp.zeros((rank, width), F32),
    )
    own = pl.ds(pl.multiple_of(chan * width, width), width)
    for s in range(shares):
        part = slice(s * width, (s + 1) * width)
        halves[s, 0:rank] = jnp.dot(
            coef, mix_ref[own, part], precision=EXACT, preferred_element_type=F32
        )
        halves[s, rank : 2 * rank] = lax.dot_general(
            total,
            mix_ref[part, own],
            (((1,), (1,)), ((), ())),
            precision=EXACT,
            preferred_element_type=F32,
        )

    copies = []
    for step in range(1, shares):
        other = lax.rem(chan + step, shares)
        copies.append(
            pltpu.make_async_remote_copy(
                src_ref=halves.at[other],
                dst_ref=joined.at[step - 1],
                send_sem=send_half.at[step],
                recv_sem=recv_half.at[step],
                device_id=(me, other),
                device_id_type=pl.DeviceIdType.MESH,
            )
        )
        copies[-1].start()
    both = halves[chan]
    for step, copy in enumerate(copies):
        copy.wait()
        both += joined[step]
    far_out[...] = both[0:rank].astype(BF16)
    back_out[...] = both[rank : 2 * rank].astype(BF16)


def backward_kernel(target_ref, tile_ref, dy_ref, left_ref, own_ref, total):
    step = pl.program_id(0)
    blocks = left_ref.shape[0]
    slots, panels = tile_ref.shape[1], tile_ref.shape[2]

    @pl.when(step == 0)
    def _():
        @pl.loop(0, 2 * blocks + 1)
        def _(row):
            total[row] = jnp.zeros(total.shape[1:], F32)

    for i in range(STEP):
        turned = dy_ref[i].T
        first = (step * STEP + i) * slots
        for k in range(0, slots, 2):
            pair = jnp.concatenate([tile_ref[i, k], tile_ref[i, k + 1]], axis=1)
            term = jnp.dot(turned, pair, preferred_element_type=F32)
            total[target_ref[first + k]] += term[:, :panels]
            total[target_ref[first + k + 1]] += term[:, panels:]

    @pl.when(step == pl.num_programs(0) - 1)
    def _():
        @pl.loop(0, blocks)
        def _(row):
            left_ref[row] = total[row].astype(BF16)
            own_ref[row] = total[blocks + row]


def forward_kernel(source_ref, tile_ref, before_ref, x_ref, bout_ref, far_ref, out_ref, held):
    step = pl.program_id(0)
    blocks = x_ref.shape[0]
    slots = tile_ref.shape[1]

    @pl.when(step == 0)
    def _():
        @pl.loop(0, blocks)
        def _(row):
            held[row] = before_ref[row]
            held[blocks + row] = x_ref[row]

        held[2 * blocks] = jnp.zeros(held.shape[1:], BF16)

    far = far_ref[...]
    for i in range(STEP):
        first = (step * STEP + i) * slots
        tiles = jnp.concatenate([tile_ref[i, k] for k in range(slots)], axis=1)
        rows = jnp.concatenate([held[source_ref[first + k]] for k in range(slots)], axis=0)
        near = jnp.dot(tiles, rows, preferred_element_type=F32)
        near += jnp.dot(bout_ref[i], far, preferred_element_type=F32)
        out_ref[i] = near.astype(BF16)


def gradient_kernel(own_ref, arrived_ref, bin_ref, back_ref, out_ref):
    back = back_ref[...]
    panels = bin_ref.shape[2]
    row = lax.broadcasted_iota(jnp.int32, (panels, panels), 0)
    col = lax.broadcasted_iota(jnp.int32, (panels, panels), 1)
    eye = jnp.where(row == col, 1.0, 0.0).astype(BF16)
    twice = jnp.concatenate([eye, eye], axis=1)
    for i in range(own_ref.shape[0]):
        turned = own_ref[i] + arrived_ref[i].astype(F32)
        high = turned.astype(BF16)
        low = (turned - high.astype(F32)).astype(BF16)
        grad = lax.dot_general(
            twice,
            jnp.concatenate([high, low], axis=1),
            (((1,), (1,)), ((), ())),
            preferred_element_type=F32,
        )
        grad += lax.dot_general(
            bin_ref[i], back, (((0,), (0,)), ((), ())), preferred_element_type=F32
        )
        out_ref[i] = grad.astype(BF16)


def body(
    features,
    cotangent,
    near_kernel,
    near_index,
    near_count,
    basis_in,
    basis_out,
    far_kernel,
    far_index,
    channel_mix,
):
    blocks, slots, panels, _ = near_kernel.shape
    width = features.shape[1]
    rank = basis_in.shape[1]
    position = lax.axis_index("curve")
    x = features.reshape(blocks, panels, width)
    dy = cotangent.reshape(blocks, panels, width)
    before = shifted(features, "curve", 1).reshape(blocks, panels, width)
    live_slot = lax.iota(jnp.int32, slots)[None, :] < near_count[:, None]
    rows = near_index - (position * blocks - blocks)
    rows = jnp.where(live_slot, rows, 2 * blocks).reshape(-1)
    tile_shape = (panels, width)
    steps = (blocks // STEP,)

    def by_step(*shape):
        zeros = (0,) * (len(shape) - 1)
        return pl.BlockSpec(shape, lambda n, *_: (n,) + zeros)

    smem = pl.BlockSpec(memory_space=pltpu.SMEM)
    vmem = pl.BlockSpec(memory_space=pltpu.VMEM)
    groups, shares = lax.axis_size("curve"), lax.axis_size("chan")
    outgoing = pl.pallas_call(
        bundle_kernel,
        out_shape=jax.ShapeDtypeStruct((groups, 2 * rank, width), BF16),
        in_specs=[smem] + [vmem] * 5,
        out_specs=vmem,
        compiler_params=params(),
        name="bundle",
    )(far_index[0], x, dy, basis_in, basis_out, far_kernel[0])

    half_flops = 2 * blocks * slots * panels * panels * width
    tile_bytes = 2 * near_kernel.size
    left, own = pl.pallas_call(
        backward_kernel,
        out_shape=(
            jax.ShapeDtypeStruct((blocks, width, panels), BF16),
            jax.ShapeDtypeStruct((blocks, width, panels), F32),
        ),
        grid_spec=pltpu.PrefetchScalarGridSpec(
            num_scalar_prefetch=1,
            grid=steps,
            in_specs=[by_step(STEP, slots, panels, panels), by_step(STEP, *tile_shape)],
            out_specs=(cover((blocks, width, panels)), cover((blocks, width, panels))),
            scratch_shapes=[pltpu.VMEM((2 * blocks + 1, width, panels), F32)],
        ),
        compiler_params=params(),
        cost_estimate=pl.CostEstimate(
            flops=4 * half_flops, bytes_accessed=2 * tile_bytes, transcendentals=0
        ),
        name="backward",
    )(rows, near_kernel, dy)
    arrived = shifted(left, "curve", -1)

    far_low, back_low = pl.pallas_call(
        functools.partial(exchange_kernel, groups, shares),
        out_shape=(jax.ShapeDtypeStruct((rank, width), BF16),) * 2,
        in_specs=[smem] + [vmem] * 3,
        out_specs=(vmem, vmem),
        scratch_shapes=[
            pltpu.VMEM((groups, 2 * rank, width), BF16),
            pltpu.VMEM((shares, 2 * rank, width), F32),
            pltpu.VMEM((max(1, shares - 1), 2 * rank, width), F32),
            pltpu.SemaphoreType.DMA((groups,)),
            pltpu.SemaphoreType.DMA((groups,)),
            pltpu.SemaphoreType.DMA((shares,)),
            pltpu.SemaphoreType.DMA((shares,)),
        ],
        compiler_params=pltpu.CompilerParams(
            collective_id=0, has_side_effects=True, vmem_limit_bytes=VMEM_LIMIT
        ),
        name="exchange",
    )(far_index[0], outgoing, far_kernel[0], channel_mix)

    layer = pl.pallas_call(
        forward_kernel,
        out_shape=jax.ShapeDtypeStruct((blocks, panels, width), BF16),
        grid_spec=pltpu.PrefetchScalarGridSpec(
            num_scalar_prefetch=1,
            grid=steps,
            in_specs=[
                by_step(STEP, slots, panels, panels),
                cover((blocks, panels, width)),
                cover((blocks, panels, width)),
                by_step(STEP, panels, rank),
                cover((rank, width)),
            ],
            out_specs=by_step(STEP, *tile_shape),
            scratch_shapes=[pltpu.VMEM((2 * blocks + 1, panels, width), BF16)],
        ),
        compiler_params=params(58),
        cost_estimate=pl.CostEstimate(
            flops=4 * half_flops, bytes_accessed=2 * tile_bytes, transcendentals=0
        ),
        name="forward",
    )(rows, near_kernel, before, x, basis_out, far_low)

    grad = pl.pallas_call(
        gradient_kernel,
        out_shape=jax.ShapeDtypeStruct((blocks, panels, width), BF16),
        grid=steps,
        in_specs=[
            by_step(STEP, width, panels),
            by_step(STEP, width, panels),
            by_step(STEP, rank, panels),
            cover((rank, width)),
        ],
        out_specs=by_step(STEP, *tile_shape),
        compiler_params=params(52),
        name="gradient",
    )(own, arrived, basis_in, back_low)
    return (layer.reshape(blocks * panels, width), grad.reshape(blocks * panels, width))


def solution(mesh):
    return jax.shard_map(
        body,
        mesh=mesh,
        in_specs=(
            P("curve", "chan"),
            P("curve", "chan"),
            P("curve", None, None, None),
            P("curve", None),
            P("curve"),
            P("curve", None, None),
            P("curve", None, None),
            P("curve", None, None, None),
            P("curve", None),
            P(),
        ),
        out_specs=(P("curve", "chan"), P("curve", "chan")),
        check_vma=False,
    )
```

time: 116 us -> 62.2 us (0.54)
  blocking collectives: 73.7 us -> 0 us
  Pallas kernels: 21.4 us -> 53.2 us
  local copies, waits for them, and re-layouts: 14.1 us -> 3.06 us
    all_gather x1 -> x0, blocking collectives: 73.7 us -> none  [body(): every = lax.all_gather(own_bundle, ('curve', 'chan'), axis=0)]
    pallas_call x2, Pallas kernels: 1.8 us -> 25.8 us  [the longest x1 22.1 us: body(): pl.pallas_call(functools.partial(exchange_kernel, groups, shares), out_sh...]
    unnamed x23 -> x9, local copies, waits for them, and re-layouts: 13.7 us -> 2.31 us
    pallas_call x1, Pallas kernels: 6.38 us -> 10.8 us  [body(): pl.pallas_call(backward_kernel, out_shape=(jax.ShapeDtypeStruct((blocks,...]
    pallas_call x1, Pallas kernels: 6.96 us -> 9.97 us  [body(): pl.pallas_call(forward_kernel, out_shape=jax.ShapeDtypeStruct((blocks, pa...]
  transfers between devices with their start and end apart: 2 -> 2, of which waited for: 0 -> 0; matrix products, arithmetic and copies ran while one was open for 2% -> 5% of each run, Pallas kernels for 13% -> 76%
where the time goes in v2:
time: 62.2 us; the launch traced here: 61.5 us
  Pallas kernels  53.2 us (86%)
  starting transfers between devices  3.84 us (6%)
  local copies, waits for them, and re-layouts  3.06 us (5%)
  between operations  0.72 us (1%)
  other arithmetic  0.69 us (1%)
    pallas_call x1, Pallas kernels, body(): pl.pallas_call(functools.partial(exchange_kernel, groups, shares), out_sh...  22.1 us
    pallas_call x1, Pallas kernels, body(): pl.pallas_call(backward_kernel, out_shape=(jax.ShapeDtypeStruct((blocks,...  10.8 us
    pallas_call x1, Pallas kernels, body(): pl.pallas_call(forward_kernel, out_shape=jax.ShapeDtypeStruct((blocks, pa...  9.97 us
    pallas_call x1, Pallas kernels, body(): pl.pallas_call(gradient_kernel, out_shape=jax.ShapeDtypeStruct((blocks, p...  6.64 us
    ppermute x2, starting transfers between devices, shifted(): lax.ppermute(value, axis, [(source, source + steps) for source in range(l...  3.84 us
    pallas_call x1, Pallas kernels, body(): pl.pallas_call(bundle_kernel, out_shape=jax.ShapeDtypeStruct((groups, 2 *...  3.69 us
    unnamed x9, local copies, waits for them, and re-layouts  2.31 us
  transfers between devices with their start and end apart: 2, of which 0 were waited for; matrix products, arithmetic and copies ran while one was open for 5% of the time, Pallas kernels for 76%

profile of v2, /device:TPU:0, one launch (start us, length us, event | category | flops | bytes accessed | tf_op | source)
XLA Modules:
  0.0 61.5 jit_solution(12511268710992052789)
XLA Ops:
  0.6 0.0 copy-start.2
  0.6 2.6 %collective-permute-start = (bf16[4096,128]{1,0:T(8,128)(2,1)}, bf16[4096,128]{1,0:T(8,128)(2,1)S(1)}, u32[]{:S(2)}, u32[]{:S(2)}) collective-permute-start(bf16[4096,128]{1,0:T(8,128)(2,1)} %param.10), channel_id=1, source_target_pairs={{0,2},{2,4},{4,6},{6,8},{8,10},{10,12},{12,14},{14,16},{16,18},{18... | collective-permute-start | bytes 3145736 | tf_op jit(solution)/shard_map/ppermute | solution.py:20
  3.2 0.7 %subtract_select_fusion = s32[32,8]{0,1:T(8,128)S(1)} fusion(s32[32,8]{0,1:T(8,128)} %param.13, s32[]{:T(128)S(6)} %sub.9, s32[32]{0:T(128)} %param.14), kind=kLoop, calls=%fused_computation | loop fusion | flops 768 | bytes 2180 | tf_op jit(solution)/shard_map/jit(_where)/select_n | solution.py:253
  3.9 0.1 copy.14
  4.0 0.7 %reshape.23.source_ref.target_ref = s32[256]{0:T(256)} reshape(s32[32,8]{1,0:T(8,128)S(1)} %copy.14) | data formatting | bytes 2048 | tf_op jit(solution)/shard_map/reshape | solution.py:253
  4.7 10.8 %backward.1 = (bf16[32,128,128]{2,1,0:T(8,128)(2,1)}, f32[32,128,128]{2,1,0:T(8,128)}) custom-call(s32[256]{0:T(256)} %reshape.23.source_ref.target_ref, bf16[32,8,128,128]{3,2,1,0:T(8,128)(2,1)} %tile_ref.3, bf16[32,128,128]{2,1,0:T(8,128)(2,1)} %bitcast.8), custom_call_target="tpu_custom_call" | custom-call | flops 4294967296 | bytes 16777216 | tf_op jit(solution)/shard_map/backward/pallas_call | solution.py:275
  15.4 1.3 %collective-permute-start.1 = (bf16[32,128,128]{2,1,0:T(8,128)(2,1)}, bf16[32,128,128]{2,1,0:T(8,128)(2,1)S(1)}, u32[]{:S(2)}, u32[]{:S(2)}) collective-permute-start(bf16[32,128,128]{2,1,0:T(8,128)(2,1)} %get-tuple-element.8), channel_id=1, source_target_pairs={{2,0},{4,2},{6,4},{8,6},{10,8},{12,10},{14,12},{16,14},{18,16},{20... | collective-permute-start | bytes 3145736 | tf_op jit(solution)/shard_map/ppermute | solution.py:20
  16.7 0.0 copy-done.2
  16.7 1.3 %copy.16.bout_ref = bf16[32,128,16]{2,1,0:T(8,128)(2,1)} copy(bf16[32,128,16]{1,2,0:T(8,128)(2,1)S(1)} %copy-done.2) | data formatting | bytes 262144 | tf_op args[6]
  18.1 3.7 %bundle.1.send_ref = bf16[16,32,128]{2,1,0:T(8,128)(2,1)} custom-call(s32[8]{0:T(128)} %bitcast.14, bf16[32,128,128]{2,1,0:T(8,128)(2,1)} %bitcast.10, bf16[32,128,128]{2,1,0:T(8,128)(2,1)} %bitcast.9, bf16[32,16,128]{2,1,0:T(8,128)(2,1)} %bin_ref.3, bf16[32,128,16]{2,1,0:T(8,128)(2,1)} %copy.16.bout_ref, f32[8,16,16]{2,1,0:T(8,128)} %bitcast.12), custom_call_target="tpu_custom_call" | custom-call | tf_op jit(solution)/shard_map/bundle/pallas_call | solution.py:264
  21.7 0.0 copy-start
  21.8 22.1 %exchange.1 = (bf16[16,128]{1,0:T(8,128)(2,1)}, bf16[16,128]{1,0:T(8,128)(2,1)}) custom-call(s32[8]{0:T(128)} %bitcast.15, bf16[16,32,128]{2,1,0:T(8,128)(2,1)} %bundle.1.send_ref, f32[8,16,16]{2,1,0:T(8,128)} %bitcast.13, f32[256,256]{1,0:T(8,128)} %mix_ref.1), custom_call_target="tpu_custom_call" | custom-call | tf_op jit(solution)/shard_map/exchange/pallas_call | solution.py:296
  43.9 0.0 copy-start.1
  43.9 0.0 collective-permute-done
  43.9 0.0 copy-start.3
  43.9 1.0 %copy-done.3 = bf16[4096,128]{1,0:T(8,128)(2,1)} copy-done((bf16[4096,128]{1,0:T(8,128)(2,1)}, bf16[4096,128]{1,0:T(8,128)(2,1)S(1)}, u32[]{:S(2)}) %copy-start.3) | copy-done | bytes 1048600
  44.9 10.0 %forward.1 = bf16[32,128,128]{2,1,0:T(8,128)(2,1)} custom-call(s32[256]{0:T(256)} %reshape.23.source_ref.target_ref, bf16[32,8,128,128]{3,2,1,0:T(8,128)(2,1)} %tile_ref.3, bf16[32,128,128]{2,1,0:T(8,128)(2,1)} %bitcast.16, bf16[32,128,128]{2,1,0:T(8,128)(2,1)} %bitcast.11, bf16[32,128,16]{2,1,0:T(8,128)(2,1)} %copy.16.bout_ref, ...), custom_call_target="tpu_custom_call" | custom-call | flops 4294967296 | bytes 16777216 | tf_op jit(solution)/shard_map/forward/pallas_call | solution.py:316
  54.9 0.0 collective-permute-done.1.arrived_ref
  54.9 0.0 copy-done
  54.9 0.0 copy-done.1
  54.9 6.6 %gradient.1 = bf16[32,128,128]{2,1,0:T(8,128)(2,1)} custom-call(f32[32,128,128]{2,1,0:T(8,128)} %get-tuple-element.7.own_ref, bf16[32,128,128]{2,1,0:T(8,128)(2,1)S(1)} %collective-permute-done.1.arrived_ref, bf16[32,16,128]{2,1,0:T(8,128)(2,1)S(1)} %copy-done, bf16[16,128]{1,0:T(8,128)(2,1)S(1)} %copy-done.1), custom_call_target="tpu_custom_call" | custom-call | tf_op jit(solution)/shard_map/gradient/pallas_call | solution.py:339
Async XLA Ops:
  0.6 16.1 %copy-start.2 = (bf16[32,128,16]{1,2,0:T(8,128)(2,1)S(1)}, bf16[32,128,16]{1,2,0:T(8,128)(2,1)}, u32[]{:S(2)}) copy-start(bf16[32,128,16]{1,2,0:T(8,128)(2,1)} %param.16) | copy-start | bytes 393220
  0.6 43.3 %collective-permute-start = (bf16[4096,128]{1,0:T(8,128)(2,1)}, bf16[4096,128]{1,0:T(8,128)(2,1)S(1)}, u32[]{:S(2)}, u32[]{:S(2)}) collective-permute-start(bf16[4096,128]{1,0:T(8,128)(2,1)} %param.10), channel_id=1, source_target_pairs={{0,2},{2,4},{4,6},{6,8},{8,10},{10,12},{12,14},{14,16},{16,18},{18... | collective-permute-start | bytes 3145736 | tf_op jit(solution)/shard_map/ppermute | solution.py:20
  15.4 39.4 %collective-permute-start.1 = (bf16[32,128,128]{2,1,0:T(8,128)(2,1)}, bf16[32,128,128]{2,1,0:T(8,128)(2,1)S(1)}, u32[]{:S(2)}, u32[]{:S(2)}) collective-permute-start(bf16[32,128,128]{2,1,0:T(8,128)(2,1)} %get-tuple-element.8), channel_id=1, source_target_pairs={{2,0},{4,2},{6,4},{8,6},{10,8},{12,10},{14,12},{16,14},{18,16},{20... | collective-permute-start | bytes 3145736 | tf_op jit(solution)/shard_map/ppermute | solution.py:20
  21.7 33.1 %copy-start = (bf16[32,16,128]{2,1,0:T(8,128)(2,1)S(1)}, bf16[32,16,128]{2,1,0:T(8,128)(2,1)}, u32[]{:S(2)}) copy-start(bf16[32,16,128]{2,1,0:T(8,128)(2,1)} %bin_ref.3) | copy-start | bytes 393220
  43.9 11.0 %copy-start.1 = (bf16[16,128]{1,0:T(8,128)(2,1)S(1)}, bf16[16,128]{1,0:T(8,128)(2,1)}, u32[]{:S(2)}) copy-start(bf16[16,128]{1,0:T(8,128)(2,1)} %get-tuple-element.9.back_ref) | copy-start | bytes 12292
  43.9 1.0 %copy-start.3 = (bf16[4096,128]{1,0:T(8,128)(2,1)}, bf16[4096,128]{1,0:T(8,128)(2,1)S(1)}, u32[]{:S(2)}) copy-start(bf16[4096,128]{1,0:T(8,128)(2,1)S(1)} %collective-permute-done) | copy-start | bytes 3145732

commit v3 on v2

--- a/solution.py
+++ b/solution.py
@@ -10,7 +10,6 @@
 F32 = jnp.float32
 BF16 = jnp.bfloat16
 EXACT = lax.Precision.HIGHEST
-VMEM_LIMIT = 60 * 1024 * 1024
 STEP = 4
 
 
@@ -36,9 +35,7 @@
     dfar = jnp.zeros((rank, width), F32)
     for b in range(blocks):
         coarse += jnp.dot(bin_ref[b], x_ref[b], preferred_element_type=F32)
-        dfar += lax.dot_general(
-            bout_ref[b], dy_ref[b], (((0,), (0,)), ((), ())), preferred_element_type=F32
-        )
+        dfar += jnp.dot(bout_ref[b], dy_ref[b], preferred_element_type=F32)
     coarse = coarse.astype(BF16)
     spread = [
         lax.dot_general(
@@ -154,56 +151,85 @@
     back_out[...] = both[rank : 2 * rank].astype(BF16)
 
 
-def backward_kernel(target_ref, tile_ref, dy_ref, left_ref, own_ref, total):
-    step = pl.program_id(0)
-    blocks = left_ref.shape[0]
-    slots, panels = tile_ref.shape[1], tile_ref.shape[2]
-
-    @pl.when(step == 0)
-    def _():
-        @pl.loop(0, 2 * blocks + 1)
-        def _(row):
-            total[row] = jnp.zeros(total.shape[1:], F32)
-
-    for i in range(STEP):
-        turned = dy_ref[i].T
-        first = (step * STEP + i) * slots
-        for k in range(0, slots, 2):
-            pair = jnp.concatenate([tile_ref[i, k], tile_ref[i, k + 1]], axis=1)
-            term = jnp.dot(turned, pair, preferred_element_type=F32)
-            total[target_ref[first + k]] += term[:, :panels]
-            total[target_ref[first + k + 1]] += term[:, panels:]
-
-    @pl.when(step == pl.num_programs(0) - 1)
-    def _():
-        @pl.loop(0, blocks)
-        def _(row):
-            left_ref[row] = total[row].astype(BF16)
-            own_ref[row] = total[blocks + row]
-
-
-def forward_kernel(source_ref, tile_ref, before_ref, x_ref, bout_ref, far_ref, out_ref, held):
-    step = pl.program_id(0)
-    blocks = x_ref.shape[0]
-    slots = tile_ref.shape[1]
-
-    @pl.when(step == 0)
-    def _():
-        @pl.loop(0, blocks)
-        def _(row):
-            held[row] = before_ref[row]
-            held[blocks + row] = x_ref[row]
-
-        held[2 * blocks] = jnp.zeros(held.shape[1:], BF16)
-
+def slot_row(index_ref, count_ref, blocks, block, slot):
+    base = lax.axis_index("curve") * blocks - blocks
+    row = index_ref[slot, block] - base
+    return jnp.where(slot < count_ref[block], row, 2 * blocks)
+
+
+def chunk_copy(hbm_ref, vmem_ref, sem, chunk):
+    rows = pl.ds(chunk * STEP, STEP)
+    return pltpu.make_async_copy(hbm_ref.at[rows], vmem_ref.at[rows], sem.at[chunk])
+
+
+def backward_kernel(index_ref, count_ref, tile_hbm, dy_ref, left_ref, own_ref, tiles, total, sem):
+    blocks, slots, panels, _ = tiles.shape
+    chunks = blocks // STEP
+    for chunk in range(chunks):
+        chunk_copy(tile_hbm, tiles, sem, chunk).start()
+
+    @pl.loop(0, 2 * blocks + 1)
+    def _(row):
+        total[row] = jnp.zeros(total.shape[1:], F32)
+
+    @pl.loop(0, chunks)
+    def _(chunk):
+        chunk_copy(tile_hbm, tiles, sem, chunk).wait()
+        for i in range(STEP):
+            block = chunk * STEP + i
+            turned = dy_ref[block].T
+            for k in range(0, slots, 2):
+                pair = jnp.concatenate([tiles[block, k], tiles[block, k + 1]], axis=1)
+                term = jnp.dot(turned, pair, preferred_element_type=F32)
+                for half in range(2):
+                    row = slot_row(index_ref, count_ref, blocks, block, k + half)
+                    total[row] += term[:, half * panels : (half + 1) * panels]
+
+    @pl.loop(0, blocks)
+    def _(row):
+        left_ref[row] = total[row].astype(BF16)
+        own_ref[row] = total[blocks + row]
+
+
+def forward_kernel(
+    index_ref, count_ref, tile_hbm, before_hbm, x_hbm, bout_ref, far_ref, out_hbm,
+    tiles, held, result, sem, held_sem, out_sem,
+):
+    blocks, slots, panels, _ = tiles.shape
+    chunks = blocks // STEP
+    loads = [
+        pltpu.make_async_copy(x_hbm, held.at[pl.ds(blocks, blocks)], held_sem.at[0]),
+        pltpu.make_async_copy(before_hbm, held.at[pl.ds(0, blocks)], held_sem.at[1]),
+    ]
+    for load in loads:
+        load.start()
+    for chunk in range(chunks):
+        chunk_copy(tile_hbm, tiles, sem, chunk).start()
+    held[2 * blocks] = jnp.zeros(held.shape[1:], BF16)
+    for load in loads:
+        load.wait()
     far = far_ref[...]
-    for i in range(STEP):
-        first = (step * STEP + i) * slots
-        tiles = jnp.concatenate([tile_ref[i, k] for k in range(slots)], axis=1)
-        rows = jnp.concatenate([held[source_ref[first + k]] for k in range(slots)], axis=0)
-        near = jnp.dot(tiles, rows, preferred_element_type=F32)
-        near += jnp.dot(bout_ref[i], far, preferred_element_type=F32)
-        out_ref[i] = near.astype(BF16)
+
+    @pl.loop(0, chunks)
+    def _(chunk):
+        chunk_copy(tile_hbm, tiles, sem, chunk).wait()
+        for i in range(STEP):
+            block = chunk * STEP + i
+            left = jnp.concatenate([tiles[block, k] for k in range(slots)], axis=1)
+            right = jnp.concatenate(
+                [held[slot_row(index_ref, count_ref, blocks, block, k)] for k in range(slots)],
+                axis=0,
+            )
+            near = jnp.dot(left, right, preferred_element_type=F32)
+            near += lax.dot_general(
+                bout_ref[block], far, (((0,), (0,)), ((), ())), preferred_element_type=F32
+            )
+            result[block] = near.astype(BF16)
+        chunk_copy(result, out_hbm, out_sem, chunk).start()
+
+    @pl.loop(0, chunks)
+    def _(chunk):
+        chunk_copy(result, out_hbm, out_sem, chunk).wait()
 
 
 def gradient_kernel(own_ref, arrived_ref, bin_ref, back_ref, out_ref):
@@ -244,15 +270,14 @@
     blocks, slots, panels, _ = near_kernel.shape
     width = features.shape[1]
     rank = basis_in.shape[1]
-    position = lax.axis_index("curve")
     x = features.reshape(blocks, panels, width)
     dy = cotangent.reshape(blocks, panels, width)
     before = shifted(features, "curve", 1).reshape(blocks, panels, width)
-    live_slot = lax.iota(jnp.int32, slots)[None, :] < near_count[:, None]
-    rows = near_index - (position * blocks - blocks)
-    rows = jnp.where(live_slot, rows, 2 * blocks).reshape(-1)
+    slot_index = near_index.T
+    bout_turned = basis_out.transpose(0, 2, 1)
     tile_shape = (panels, width)
-    steps = (blocks // STEP,)
+    part = blocks // 2
+    chunks = blocks // STEP
 
     def by_step(*shape):
         zeros = (0,) * (len(shape) - 1)
@@ -260,15 +285,17 @@
 
     smem = pl.BlockSpec(memory_space=pltpu.SMEM)
     vmem = pl.BlockSpec(memory_space=pltpu.VMEM)
+    anywhere = pl.BlockSpec(memory_space=pl.ANY)
+    hbm = pl.BlockSpec(memory_space=pltpu.MemorySpace.HBM)
     groups, shares = lax.axis_size("curve"), lax.axis_size("chan")
     outgoing = pl.pallas_call(
         bundle_kernel,
         out_shape=jax.ShapeDtypeStruct((groups, 2 * rank, width), BF16),
         in_specs=[smem] + [vmem] * 5,
         out_specs=vmem,
-        compiler_params=params(),
+        compiler_params=params(60),
         name="bundle",
-    )(far_index[0], x, dy, basis_in, basis_out, far_kernel[0])
+    )(far_index[0], x, dy, basis_in, bout_turned, far_kernel[0])
 
     half_flops = 2 * blocks * slots * panels * panels * width
     tile_bytes = 2 * near_kernel.size
@@ -278,21 +305,21 @@
             jax.ShapeDtypeStruct((blocks, width, panels), BF16),
             jax.ShapeDtypeStruct((blocks, width, panels), F32),
         ),
-        grid_spec=pltpu.PrefetchScalarGridSpec(
-            num_scalar_prefetch=1,
-            grid=steps,
-            in_specs=[by_step(STEP, slots, panels, panels), by_step(STEP, *tile_shape)],
-            out_specs=(cover((blocks, width, panels)), cover((blocks, width, panels))),
-            scratch_shapes=[pltpu.VMEM((2 * blocks + 1, width, panels), F32)],
-        ),
-        compiler_params=params(),
+        in_specs=[smem, smem, hbm, vmem],
+        out_specs=(vmem, vmem),
+        scratch_shapes=[
+            pltpu.VMEM((blocks, slots, panels, panels), BF16),
+            pltpu.VMEM((2 * blocks + 1, width, panels), F32),
+            pltpu.SemaphoreType.DMA((chunks,)),
+        ],
+        compiler_params=params(57),
         cost_estimate=pl.CostEstimate(
             flops=4 * half_flops, bytes_accessed=2 * tile_bytes, transcendentals=0
         ),
         name="backward",
-    )(rows, near_kernel, dy)
-    arrived = shifted(left, "curve", -1)
-
+    )(slot_index, near_count, near_kernel, dy)
+
+    left, outgoing = lax.optimization_barrier((left, outgoing))
     far_low, back_low = pl.pallas_call(
         functools.partial(exchange_kernel, groups, shares),
         out_shape=(jax.ShapeDtypeStruct((rank, width), BF16),) * 2,
@@ -308,46 +335,45 @@
             pltpu.SemaphoreType.DMA((shares,)),
         ],
         compiler_params=pltpu.CompilerParams(
-            collective_id=0, has_side_effects=True, vmem_limit_bytes=VMEM_LIMIT
+            collective_id=0, has_side_effects=True, vmem_limit_bytes=40 * 1024 * 1024
         ),
         name="exchange",
     )(far_index[0], outgoing, far_kernel[0], channel_mix)
+    left, far_low = lax.optimization_barrier((left, far_low))
+    arrived = shifted(left, "curve", -1)
 
     layer = pl.pallas_call(
         forward_kernel,
         out_shape=jax.ShapeDtypeStruct((blocks, panels, width), BF16),
-        grid_spec=pltpu.PrefetchScalarGridSpec(
-            num_scalar_prefetch=1,
-            grid=steps,
-            in_specs=[
-                by_step(STEP, slots, panels, panels),
-                cover((blocks, panels, width)),
-                cover((blocks, panels, width)),
-                by_step(STEP, panels, rank),
-                cover((rank, width)),
-            ],
-            out_specs=by_step(STEP, *tile_shape),
-            scratch_shapes=[pltpu.VMEM((2 * blocks + 1, panels, width), BF16)],
-        ),
-        compiler_params=params(58),
+        in_specs=[smem, smem, hbm, anywhere, anywhere, vmem, vmem],
+        out_specs=hbm,
+        scratch_shapes=[
+            pltpu.VMEM((blocks, slots, panels, panels), BF16),
+            pltpu.VMEM((2 * blocks + 1, panels, width), BF16),
+            pltpu.VMEM((blocks, panels, width), BF16),
+            pltpu.SemaphoreType.DMA((chunks,)),
+            pltpu.SemaphoreType.DMA((2,)),
+            pltpu.SemaphoreType.DMA((chunks,)),
+        ],
+        compiler_params=params(40),
         cost_estimate=pl.CostEstimate(
             flops=4 * half_flops, bytes_accessed=2 * tile_bytes, transcendentals=0
         ),
         name="forward",
-    )(rows, near_kernel, before, x, basis_out, far_low)
+    )(slot_index, near_count, near_kernel, before, x, bout_turned, far_low)
 
     grad = pl.pallas_call(
         gradient_kernel,
         out_shape=jax.ShapeDtypeStruct((blocks, panels, width), BF16),
-        grid=steps,
+        grid=(2,),
         in_specs=[
-            by_step(STEP, width, panels),
-            by_step(STEP, width, panels),
-            by_step(STEP, rank, panels),
+            by_step(part, width, panels),
+            by_step(part, width, panels),
+            by_step(part, rank, panels),
             cover((rank, width)),
         ],
-        out_specs=by_step(STEP, *tile_shape),
-        compiler_params=params(52),
+        out_specs=by_step(part, *tile_shape),
+        compiler_params=params(40),
         name="gradient",
     )(own, arrived, basis_in, back_low)
     return (layer.reshape(blocks * panels, width), grad.reshape(blocks * panels, width))

time: 62.2 us -> 48.1 us (0.77)
  the two profiles are of different devices: /device:TPU:0 before, /device:TPU:1 now
where the time goes in v3:
time: 48.1 us; the launch traced here: 47.9 us
  Pallas kernels  31.8 us (66%)
  starting transfers between devices  7.58 us (16%)
  waiting for transfers between devices  4.3 us (9%)
  local copies, waits for them, and re-layouts  3.43 us (7%)
  between operations  0.81 us (2%)
    pallas_call x1, Pallas kernels, body(): pl.pallas_call(functools.partial(exchange_kernel, groups, shares), out_sh...  11.3 us
    pallas_call x1, Pallas kernels, body(): pl.pallas_call(backward_kernel, out_shape=(jax.ShapeDtypeStruct((blocks,...  8.79 us
    ppermute x2, starting transfers between devices, shifted(): lax.ppermute(value, axis, [(source, source + steps) for source in range(l...  7.58 us
    pallas_call x1, Pallas kernels, body(): pl.pallas_call(forward_kernel, out_shape=jax.ShapeDtypeStruct((blocks, pa...  6.09 us
    ppermute x2, waiting for transfers between devices, shifted(): lax.ppermute(value, axis, [(source, source + steps) for source in range(l...  4.3 us
    unnamed x22, local copies, waits for them, and re-layouts  3.43 us
    pallas_call x1, Pallas kernels, body(): pl.pallas_call(bundle_kernel, out_shape=jax.ShapeDtypeStruct((groups, 2 *...  3.38 us
    pallas_call x1, Pallas kernels, body(): pl.pallas_call(gradient_kernel, out_shape=jax.ShapeDtypeStruct((blocks, p...  2.23 us
  transfers between devices with their start and end apart: 2, of which 1 were waited for; matrix products, arithmetic and copies ran while one was open for 0% of the time, Pallas kernels for 62%

profile of v3, /device:TPU:1, one launch (start us, length us, event | category | flops | bytes accessed | tf_op | source)
XLA Modules:
  0.0 47.9 jit_solution(9262020585321556683)
XLA Ops:
  0.6 4.5 %collective-permute-start = (bf16[4096,128]{1,0:T(8,128)(2,1)}, bf16[4096,128]{1,0:T(8,128)(2,1)S(1)}, u32[]{:S(2)}, u32[]{:S(2)}) collective-permute-start(bf16[4096,128]{1,0:T(8,128)(2,1)} %param.10), channel_id=1, source_target_pairs={{0,2},{2,4},{4,6},{6,8},{8,10},{10,12},{12,14},{14,16},{16,18},{18... | collective-permute-start | bytes 3145736 | tf_op jit(solution)/shard_map/ppermute | solution.py:19
  5.2 3.4 %bundle.1.send_ref = bf16[16,32,128]{2,1,0:T(8,128)(2,1)} custom-call(s32[8]{0:T(128)} %bitcast.15, bf16[32,128,128]{2,1,0:T(8,128)(2,1)} %bitcast.9, bf16[32,128,128]{2,1,0:T(8,128)(2,1)} %bitcast.21, bf16[32,16,128]{2,1,0:T(8,128)(2,1)} %bin_ref.3, bf16[32,16,128]{2,1,0:T(8,128)(2,1)} %bitcast.13, f32[8,16,16]{2,1,0:T(8,128)} %bitcast.11), custom_call_target="tpu_custom_call" | custom-call | tf_op jit(solution)/shard_map/bundle/pallas_call | solution.py:291
  8.6 0.0 copy-start.7
  8.6 0.0 copy-start.1
  8.6 0.0 copy-start.6
  8.6 0.0 copy-start.9
  8.6 0.0 copy-start.10
  8.6 8.8 %backward.1 = (bf16[32,128,128]{2,1,0:T(8,128)(2,1)}, f32[32,128,128]{2,1,0:T(8,128)}) custom-call(s32[8,32]{1,0:T(8,128)} %bitcast.18, s32[32]{0:T(128)} %count_ref.3, bf16[32,8,128,128]{3,2,1,0:T(8,128)(2,1)} %tile_hbm.3, bf16[32,128,128]{2,1,0:T(8,128)(2,1)} %bitcast.22), custom_call_target="tpu_custom_call" | custom-call | flops 4294967296 | bytes 16777216 | tf_op jit(solution)/shard_map/backward/pallas_call | solution.py:302
  17.4 0.0 copy-start
  17.4 0.0 copy-start.2
  17.4 0.0 copy-done.3
  17.5 0.0 copy-done.4
  17.5 0.0 copy-done.5
  17.5 0.0 copy-done.7
  17.5 11.3 %exchange.1 = (bf16[16,128]{1,0:T(8,128)(2,1)S(1)}, bf16[16,128]{1,0:T(8,128)(2,1)S(1)}) custom-call(s32[8]{0:T(128)S(1)} %bitcast.16, bf16[16,32,128]{2,1,0:T(8,128)(2,1)S(1)} %copy-done.3, f32[8,16,16]{2,1,0:T(8,128)S(1)} %bitcast.12, f32[256,256]{1,0:T(8,128)S(1)} %copy-done.4), custom_call_target="tpu_custom_call" | custom-call | tf_op jit(solution)/shard_map/exchange/pallas_call | solution.py:323
  28.8 3.0 %collective-permute-start.1 = (bf16[32,128,128]{2,1,0:T(8,128)(2,1)}, bf16[32,128,128]{2,1,0:T(8,128)(2,1)S(1)}, u32[]{:S(2)}, u32[]{:S(2)}) collective-permute-start(bf16[32,128,128]{2,1,0:T(8,128)(2,1)} %get-tuple-element.16), channel_id=1, source_target_pairs={{2,0},{4,2},{6,4},{8,6},{10,8},{12,10},{14,12},{16,14},{18,16},{20... | collective-permute-start | bytes 3145736 | tf_op jit(solution)/shard_map/ppermute | solution.py:19
  31.8 0.0 collective-permute-done
  31.8 0.0 copy-done.1
  31.8 0.0 copy-done.6
  31.9 0.0 copy-start.8
  31.9 3.4 %copy-done.8 = bf16[32,8,128,128]{3,2,1,0:T(8,128)(2,1)S(1)} copy-done((bf16[32,8,128,128]{3,2,1,0:T(8,128)(2,1)S(1)}, bf16[32,8,128,128]{3,2,1,0:T(8,128)(2,1)}, u32[]{:S(2)}) %copy-start.8) | copy-done | bytes 8388632
  35.3 6.1 %forward.1 = bf16[32,128,128]{2,1,0:T(8,128)(2,1)} custom-call(s32[8,32]{1,0:T(8,128)S(1)} %bitcast.19, s32[32]{0:T(128)S(1)} %copy-done.10, bf16[32,8,128,128]{3,2,1,0:T(8,128)(2,1)S(1)} %copy-done.8, bf16[32,128,128]{2,1,0:T(8,128)(2,1)S(1)} %bitcast.17, bf16[32,128,128]{2,1,0:T(8,128)(2,1)S(1)} %bitcast.10, bf16[32,16,128]{2,1,0:T(8,128)(2,1)S(1)} %bitcast.14, ...), custom_call_target="tpu_custom_call" | custom-call | flops 4294967296 | bytes 16777216 | tf_op jit(solution)/shard_map/forward/pallas_call | solution.py:345
  41.4 4.3 %collective-permute-done.1.arrived_ref = bf16[32,128,128]{2,1,0:T(8,128)(2,1)S(1)} collective-permute-done((bf16[32,128,128]{2,1,0:T(8,128)(2,1)}, bf16[32,128,128]{2,1,0:T(8,128)(2,1)S(1)}, u32[]{:S(2)}, u32[]{:S(2)}) %collective-permute-start.1) | collective-permute-done | bytes 1048608 | tf_op jit(solution)/shard_map/ppermute | solution.py:19
  45.7 2.2 %gradient.1 = bf16[32,128,128]{2,1,0:T(8,128)(2,1)} custom-call(f32[32,128,128]{2,1,0:T(8,128)S(1)} %copy-done, bf16[32,128,128]{2,1,0:T(8,128)(2,1)S(1)} %collective-permute-done.1.arrived_ref, bf16[32,16,128]{2,1,0:T(8,128)(2,1)S(1)} %copy-done.2, bf16[16,128]{1,0:T(8,128)(2,1)S(1)} %get-tuple-element.17.back_ref), custom_call_target="tpu_custom_call" | custom-call | tf_op jit(solution)/shard_map/gradient/pallas_call | solution.py:365
  (7 shorter events, 0.0 us)
Async XLA Ops:
  0.6 31.2 %collective-permute-start = (bf16[4096,128]{1,0:T(8,128)(2,1)}, bf16[4096,128]{1,0:T(8,128)(2,1)S(1)}, u32[]{:S(2)}, u32[]{:S(2)}) collective-permute-start(bf16[4096,128]{1,0:T(8,128)(2,1)} %param.10), channel_id=1, source_target_pairs={{0,2},{2,4},{4,6},{6,8},{8,10},{10,12},{12,14},{14,16},{16,18},{18... | collective-permute-start | bytes 3145736 | tf_op jit(solution)/shard_map/ppermute | solution.py:19
  8.6 8.9 %copy-start.3 = (bf16[16,32,128]{2,1,0:T(8,128)(2,1)S(1)}, bf16[16,32,128]{2,1,0:T(8,128)(2,1)}, u32[]{:S(2)}) copy-start(bf16[16,32,128]{2,1,0:T(8,128)(2,1)} %bundle.1.send_ref) | copy-start | bytes 393220
  8.6 8.9 %copy-start.4 = (f32[256,256]{1,0:T(8,128)S(1)}, f32[256,256]{1,0:T(8,128)}, u32[]{:S(2)}) copy-start(f32[256,256]{1,0:T(8,128)} %mix_ref.1) | copy-start | bytes 786436
  8.6 8.9 %copy-start.5 = (f32[1,8,16,16]{3,2,1,0:T(8,128)S(1)}, f32[1,8,16,16]{3,2,1,0:T(8,128)}, u32[]{:S(2)}) copy-start(f32[1,8,16,16]{3,2,1,0:T(8,128)} %param.17) | copy-start | bytes 24580
  8.6 8.9 %copy-start.7 = (s32[1,8]{1,0:T(1,128)S(1)}, s32[1,8]{1,0:T(1,128)}, u32[]{:S(2)}) copy-start(s32[1,8]{1,0:T(1,128)} %param.18) | copy-start | bytes 100
  8.6 23.3 %copy-start.1 = (bf16[4096,128]{1,0:T(8,128)(2,1)S(1)}, bf16[4096,128]{1,0:T(8,128)(2,1)}, u32[]{:S(2)}) copy-start(bf16[4096,128]{1,0:T(8,128)(2,1)} %param.10) | copy-start | bytes 3145732
  8.6 23.3 %copy-start.6 = (bf16[32,128,16]{1,2,0:T(8,128)(2,1)S(1)}, bf16[32,128,16]{1,2,0:T(8,128)(2,1)}, u32[]{:S(2)}) copy-start(bf16[32,128,16]{1,2,0:T(8,128)(2,1)} %param.16) | copy-start | bytes 393220
  8.6 23.2 %copy-start.9 = (s32[32,8]{0,1:T(8,128)S(1)}, s32[32,8]{0,1:T(8,128)}, u32[]{:S(2)}) copy-start(s32[32,8]{0,1:T(8,128)} %param.13) | copy-start | bytes 3076
  8.6 23.2 %copy-start.10 = (s32[32]{0:T(128)S(1)}, s32[32]{0:T(128)}, u32[]{:S(2)}) copy-start(s32[32]{0:T(128)} %count_ref.3) | copy-start | bytes 388
  17.4 28.2 %copy-start = (f32[32,128,128]{2,1,0:T(8,128)S(1)}, f32[32,128,128]{2,1,0:T(8,128)}, u32[]{:S(2)}) copy-start(f32[32,128,128]{2,1,0:T(8,128)} %get-tuple-element.15.own_ref) | copy-start | bytes 6291460
  17.4 28.2 %copy-start.2 = (bf16[32,16,128]{2,1,0:T(8,128)(2,1)S(1)}, bf16[32,16,128]{2,1,0:T(8,128)(2,1)}, u32[]{:S(2)}) copy-start(bf16[32,16,128]{2,1,0:T(8,128)(2,1)} %bin_ref.3) | copy-start | bytes 393220
  28.8 16.9 %collective-permute-start.1 = (bf16[32,128,128]{2,1,0:T(8,128)(2,1)}, bf16[32,128,128]{2,1,0:T(8,128)(2,1)S(1)}, u32[]{:S(2)}, u32[]{:S(2)}) collective-permute-start(bf16[32,128,128]{2,1,0:T(8,128)(2,1)} %get-tuple-element.16), channel_id=1, source_target_pairs={{2,0},{4,2},{6,4},{8,6},{10,8},{12,10},{14,12},{16,14},{18,16},{20... | collective-permute-start | bytes 3145736 | tf_op jit(solution)/shard_map/ppermute | solution.py:19
  31.9 3.4 %copy-start.8 = (bf16[32,8,128,128]{3,2,1,0:T(8,128)(2,1)S(1)}, bf16[32,8,128,128]{3,2,1,0:T(8,128)(2,1)}, u32[]{:S(2)}) copy-start(bf16[32,8,128,128]{3,2,1,0:T(8,128)(2,1)} %tile_hbm.3) | copy-start | bytes 25165828

commit v4 on v3

--- a/solution.py
+++ b/solution.py
@@ -55,7 +55,7 @@
 
 def exchange_kernel(
     groups, shares, part_ref, send_ref, far_ref, mix_ref, far_out, back_out,
-    held, halves, joined, send_sem, recv_sem, send_half, recv_half,
+    held, halves, joined, turned, send_sem, recv_sem, send_half, recv_half,
 ):
     me, chan = lax.axis_index("curve"), lax.axis_index("chan")
     rank, width = far_out.shape
@@ -96,38 +96,30 @@
         along_curve(step).start()
 
     held[me] = send_ref[me]
+    own = pl.ds(pl.multiple_of(chan * width, width), width)
+    far = jnp.concatenate([far_ref[a] for a in range(partners)], axis=1)
+    high = far.astype(BF16)
+    low = (far - high.astype(F32)).astype(BF16)
+    turned[...] = mix_ref[:, own].T
 
     @pl.loop(1, groups)
     def _(step):
         along_curve(step).wait()
 
-    coef = jnp.zeros((rank, width), F32)
-    for a in range(partners):
-        far = far_ref[a]
-        high = far.astype(BF16)
-        low = (far - high.astype(F32)).astype(BF16)
-        row = held[part_ref[a], 0:rank]
-        coef += jnp.dot(high, row, preferred_element_type=F32)
-        coef += jnp.dot(low, row, preferred_element_type=F32)
+    rows = jnp.concatenate([held[part_ref[a], 0:rank] for a in range(partners)], axis=0)
+    coef = jnp.dot(high, rows, preferred_element_type=F32)
+    coef += jnp.dot(low, rows, preferred_element_type=F32)
     total = lax.fori_loop(
         0,
         groups,
         lambda g, acc: acc + held[g, rank : 2 * rank].astype(F32),
         jnp.zeros((rank, width), F32),
     )
-    own = pl.ds(pl.multiple_of(chan * width, width), width)
+    term = jnp.dot(coef, mix_ref[own, :], precision=EXACT, preferred_element_type=F32)
+    back = jnp.dot(total, turned[...], precision=EXACT, preferred_element_type=F32)
     for s in range(shares):
-        part = slice(s * width, (s + 1) * width)
-        halves[s, 0:rank] = jnp.dot(
-            coef, mix_ref[own, part], precision=EXACT, preferred_element_type=F32
-        )
-        halves[s, rank : 2 * rank] = lax.dot_general(
-            total,
-            mix_ref[part, own],
-            (((1,), (1,)), ((), ())),
-            precision=EXACT,
-            preferred_element_type=F32,
-        )
+        halves[s, 0:rank] = term[:, s * width : (s + 1) * width]
+        halves[s, rank : 2 * rank] = back[:, s * width : (s + 1) * width]
 
     copies = []
     for step in range(1, shares):
@@ -329,6 +321,7 @@
             pltpu.VMEM((groups, 2 * rank, width), BF16),
             pltpu.VMEM((shares, 2 * rank, width), F32),
             pltpu.VMEM((max(1, shares - 1), 2 * rank, width), F32),
+            pltpu.VMEM((width, shares * width), F32),
             pltpu.SemaphoreType.DMA((groups,)),
             pltpu.SemaphoreType.DMA((groups,)),
             pltpu.SemaphoreType.DMA((shares,)),
@@ -337,9 +330,12 @@
         compiler_params=pltpu.CompilerParams(
             collective_id=0, has_side_effects=True, vmem_limit_bytes=40 * 1024 * 1024
         ),
+        cost_estimate=pl.CostEstimate(
+            flops=0, bytes_accessed=4 * tile_bytes, transcendentals=0
+        ),
         name="exchange",
     )(far_index[0], outgoing, far_kernel[0], channel_mix)
-    left, far_low = lax.optimization_barrier((left, far_low))
+    left, back_low = lax.optimization_barrier((left, back_low))
     arrived = shifted(left, "curve", -1)
 
     layer = pl.pallas_call(
@@ -355,7 +351,7 @@
             pltpu.SemaphoreType.DMA((2,)),
             pltpu.SemaphoreType.DMA((chunks,)),
         ],
-        compiler_params=params(40),
+        compiler_params=params(57),
         cost_estimate=pl.CostEstimate(
             flops=4 * half_flops, bytes_accessed=2 * tile_bytes, transcendentals=0
         ),

time: 48.1 us -> 48.2 us (level)
  Pallas kernels: 31.8 us -> 34.4 us
  local copies, waits for them, and re-layouts: 3.43 us -> 1.58 us
  waiting for transfers between devices: 4.3 us -> 3.71 us
    pallas_call x1, Pallas kernels: 6.09 us -> 9.11 us  [body(): pl.pallas_call(forward_kernel, out_shape=jax.ShapeDtypeStruct((blocks, pa...]
    unnamed x22 -> x16, local copies, waits for them, and re-layouts: 3.43 us -> 1.58 us
    ppermute x2, waiting for transfers between devices: 4.3 us -> 3.71 us  [shifted(): lax.ppermute(value, axis, [(source, source + steps) for source in range(l...]
  transfers between devices with their start and end apart: 2 -> 2, of which waited for: 1 -> 1; matrix products, arithmetic and copies ran while one was open for 0% -> 0% of each run, Pallas kernels for 62% -> 67%
where the time goes in v4:
time: 48.2 us; the launch traced here: 48 us
  Pallas kernels  34.4 us (71%)
  starting transfers between devices  7.57 us (16%)
  waiting for transfers between devices  3.71 us (8%)
  local copies, waits for them, and re-layouts  1.58 us (3%)
  between operations  0.75 us (2%)
    pallas_call x1, Pallas kernels, body(): pl.pallas_call(functools.partial(exchange_kernel, groups, shares), out_sh...  11 us
    pallas_call x1, Pallas kernels, body(): pl.pallas_call(forward_kernel, out_shape=jax.ShapeDtypeStruct((blocks, pa...  9.11 us
    pallas_call x1, Pallas kernels, body(): pl.pallas_call(backward_kernel, out_shape=(jax.ShapeDtypeStruct((blocks,...  8.66 us
    ppermute x2, starting transfers between devices, shifted(): lax.ppermute(value, axis, [(source, source + steps) for source in range(l...  7.57 us
    ppermute x2, waiting for transfers between devices, shifted(): lax.ppermute(value, axis, [(source, source + steps) for source in range(l...  3.71 us
    pallas_call x1, Pallas kernels, body(): pl.pallas_call(bundle_kernel, out_shape=jax.ShapeDtypeStruct((groups, 2 *...  3.38 us
    pallas_call x1, Pallas kernels, body(): pl.pallas_call(gradient_kernel, out_shape=jax.ShapeDtypeStruct((blocks, p...  2.23 us
    unnamed x16, local copies, waits for them, and re-layouts  1.58 us
  transfers between devices with their start and end apart: 2, of which 1 were waited for; matrix products, arithmetic and copies ran while one was open for 0% of the time, Pallas kernels for 67%

profile of v4, /device:TPU:1, one launch (start us, length us, event | category | flops | bytes accessed | tf_op | source)
XLA Modules:
  0.0 48.0 jit_solution(6546478960598221108)
XLA Ops:
  0.6 4.5 %collective-permute-start = (bf16[4096,128]{1,0:T(8,128)(2,1)}, bf16[4096,128]{1,0:T(8,128)(2,1)S(1)}, u32[]{:S(2)}, u32[]{:S(2)}) collective-permute-start(bf16[4096,128]{1,0:T(8,128)(2,1)} %param.10), channel_id=1, source_target_pairs={{0,2},{2,4},{4,6},{6,8},{8,10},{10,12},{12,14},{14,16},{16,18},{18... | collective-permute-start | bytes 3145736 | tf_op jit(solution)/shard_map/ppermute | solution.py:19
  5.2 3.4 %bundle.1.send_ref = bf16[16,32,128]{2,1,0:T(8,128)(2,1)} custom-call(s32[8]{0:T(128)} %bitcast.11, bf16[32,128,128]{2,1,0:T(8,128)(2,1)} %bitcast.16, bf16[32,128,128]{2,1,0:T(8,128)(2,1)} %bitcast.14, bf16[32,16,128]{2,1,0:T(8,128)(2,1)} %bin_ref.3, bf16[32,16,128]{2,1,0:T(8,128)(2,1)} %bitcast.18, f32[8,16,16]{2,1,0:T(8,128)} %bitcast.9), custom_call_target="tpu_custom_call" | custom-call | tf_op jit(solution)/shard_map/bundle/pallas_call | solution.py:283
  8.6 0.0 copy-start.2
  8.6 0.0 copy-start.3
  8.6 0.0 copy-start.5
  8.6 8.7 %backward.1 = (bf16[32,128,128]{2,1,0:T(8,128)(2,1)}, f32[32,128,128]{2,1,0:T(8,128)}) custom-call(s32[8,32]{1,0:T(8,128)} %bitcast.21, s32[32]{0:T(128)} %count_ref.3, bf16[32,8,128,128]{3,2,1,0:T(8,128)(2,1)} %tile_hbm.3, bf16[32,128,128]{2,1,0:T(8,128)(2,1)} %bitcast.15), custom_call_target="tpu_custom_call" | custom-call | flops 4294967296 | bytes 16777216 | tf_op jit(solution)/shard_map/backward/pallas_call | solution.py:294
  17.2 0.0 copy-start
  17.3 0.0 copy-start.1
  17.3 0.0 copy-done.2
  17.3 0.0 copy-done.3
  17.3 0.0 copy-done.4
  17.3 0.0 copy-done.5
  17.3 11.0 %exchange.1 = (bf16[16,128]{1,0:T(8,128)(2,1)S(1)}, bf16[16,128]{1,0:T(8,128)(2,1)S(1)}) custom-call(s32[8]{0:T(128)S(1)} %bitcast.12, bf16[16,32,128]{2,1,0:T(8,128)(2,1)S(1)} %copy-done.2, f32[8,16,16]{2,1,0:T(8,128)S(1)} %bitcast.10, f32[256,256]{1,0:T(8,128)S(1)} %copy-done.3), custom_call_target="tpu_custom_call" | custom-call | bytes 33554432 | tf_op jit(solution)/shard_map/exchange/pallas_call | solution.py:315
  28.3 0.0 copy-start.6
  28.3 0.6 %copy-done.6 = bf16[16,128]{1,0:T(8,128)(2,1)} copy-done((bf16[16,128]{1,0:T(8,128)(2,1)}, bf16[16,128]{1,0:T(8,128)(2,1)S(1)}, u32[]{:S(2)}) %copy-start.6) | copy-done | bytes 4120
  28.9 3.0 %collective-permute-start.1 = (bf16[32,128,128]{2,1,0:T(8,128)(2,1)}, bf16[32,128,128]{2,1,0:T(8,128)(2,1)S(1)}, u32[]{:S(2)}, u32[]{:S(2)}) collective-permute-start(bf16[32,128,128]{2,1,0:T(8,128)(2,1)} %get-tuple-element.16), channel_id=1, source_target_pairs={{2,0},{4,2},{6,4},{8,6},{10,8},{12,10},{14,12},{16,14},{18,16},{20... | collective-permute-start | bytes 3145736 | tf_op jit(solution)/shard_map/ppermute | solution.py:19
  31.9 0.0 collective-permute-done
  32.0 0.0 copy-start.7
  32.0 1.0 %copy-done.7 = bf16[4096,128]{1,0:T(8,128)(2,1)} copy-done((bf16[4096,128]{1,0:T(8,128)(2,1)}, bf16[4096,128]{1,0:T(8,128)(2,1)S(1)}, u32[]{:S(2)}) %copy-start.7) | copy-done | bytes 1048600
  32.9 9.1 %forward.1 = bf16[32,128,128]{2,1,0:T(8,128)(2,1)} custom-call(s32[8,32]{1,0:T(8,128)} %bitcast.22, s32[32]{0:T(128)} %count_ref.3, bf16[32,8,128,128]{3,2,1,0:T(8,128)(2,1)} %tile_hbm.3, bf16[32,128,128]{2,1,0:T(8,128)(2,1)} %bitcast.20, bf16[32,128,128]{2,1,0:T(8,128)(2,1)} %bitcast.17, bf16[32,16,128]{2,1,0:T(8,128)(2,1)} %bitcast.19, ...), custom_call_target="tpu_custom_call" | custom-call | flops 4294967296 | bytes 16777216 | tf_op jit(solution)/shard_map/forward/pallas_call | solution.py:341
  42.0 3.7 %collective-permute-done.1.arrived_ref = bf16[32,128,128]{2,1,0:T(8,128)(2,1)S(1)} collective-permute-done((bf16[32,128,128]{2,1,0:T(8,128)(2,1)}, bf16[32,128,128]{2,1,0:T(8,128)(2,1)S(1)}, u32[]{:S(2)}, u32[]{:S(2)}) %collective-permute-start.1) | collective-permute-done | bytes 1048608 | tf_op jit(solution)/shard_map/ppermute | solution.py:19
  45.8 0.0 copy-done
  45.8 0.0 copy-done.1
  45.8 2.2 %gradient.1 = bf16[32,128,128]{2,1,0:T(8,128)(2,1)} custom-call(f32[32,128,128]{2,1,0:T(8,128)S(1)} %copy-done, bf16[32,128,128]{2,1,0:T(8,128)(2,1)S(1)} %collective-permute-done.1.arrived_ref, bf16[32,16,128]{2,1,0:T(8,128)(2,1)S(1)} %copy-done.1, bf16[16,128]{1,0:T(8,128)(2,1)S(1)} %get-tuple-element.17.back_ref), custom_call_target="tpu_custom_call" | custom-call | tf_op jit(solution)/shard_map/gradient/pallas_call | solution.py:361
  (1 shorter events, 0.0 us)
Async XLA Ops:
  0.6 31.3 %collective-permute-start = (bf16[4096,128]{1,0:T(8,128)(2,1)}, bf16[4096,128]{1,0:T(8,128)(2,1)S(1)}, u32[]{:S(2)}, u32[]{:S(2)}) collective-permute-start(bf16[4096,128]{1,0:T(8,128)(2,1)} %param.10), channel_id=1, source_target_pairs={{0,2},{2,4},{4,6},{6,8},{8,10},{10,12},{12,14},{14,16},{16,18},{18... | collective-permute-start | bytes 3145736 | tf_op jit(solution)/shard_map/ppermute | solution.py:19
  8.6 8.7 %copy-start.2 = (bf16[16,32,128]{2,1,0:T(8,128)(2,1)S(1)}, bf16[16,32,128]{2,1,0:T(8,128)(2,1)}, u32[]{:S(2)}) copy-start(bf16[16,32,128]{2,1,0:T(8,128)(2,1)} %bundle.1.send_ref) | copy-start | bytes 393220
  8.6 8.7 %copy-start.3 = (f32[256,256]{1,0:T(8,128)S(1)}, f32[256,256]{1,0:T(8,128)}, u32[]{:S(2)}) copy-start(f32[256,256]{1,0:T(8,128)} %mix_ref.1) | copy-start | bytes 786436
  8.6 8.7 %copy-start.4 = (f32[1,8,16,16]{3,2,1,0:T(8,128)S(1)}, f32[1,8,16,16]{3,2,1,0:T(8,128)}, u32[]{:S(2)}) copy-start(f32[1,8,16,16]{3,2,1,0:T(8,128)} %param.17) | copy-start | bytes 24580
  8.6 8.7 %copy-start.5 = (s32[1,8]{1,0:T(1,128)S(1)}, s32[1,8]{1,0:T(1,128)}, u32[]{:S(2)}) copy-start(s32[1,8]{1,0:T(1,128)} %param.18) | copy-start | bytes 100
  17.2 28.5 %copy-start = (f32[32,128,128]{2,1,0:T(8,128)S(1)}, f32[32,128,128]{2,1,0:T(8,128)}, u32[]{:S(2)}) copy-start(f32[32,128,128]{2,1,0:T(8,128)} %get-tuple-element.13.own_ref) | copy-start | bytes 6291460
  17.3 28.5 %copy-start.1 = (bf16[32,16,128]{2,1,0:T(8,128)(2,1)S(1)}, bf16[32,16,128]{2,1,0:T(8,128)(2,1)}, u32[]{:S(2)}) copy-start(bf16[32,16,128]{2,1,0:T(8,128)(2,1)} %bin_ref.3) | copy-start | bytes 393220
  28.3 0.6 %copy-start.6 = (bf16[16,128]{1,0:T(8,128)(2,1)}, bf16[16,128]{1,0:T(8,128)(2,1)S(1)}, u32[]{:S(2)}) copy-start(bf16[16,128]{1,0:T(8,128)(2,1)S(1)} %get-tuple-element.12.far_ref) | copy-start | bytes 12292
  28.9 16.8 %collective-permute-start.1 = (bf16[32,128,128]{2,1,0:T(8,128)(2,1)}, bf16[32,128,128]{2,1,0:T(8,128)(2,1)S(1)}, u32[]{:S(2)}, u32[]{:S(2)}) collective-permute-start(bf16[32,128,128]{2,1,0:T(8,128)(2,1)} %get-tuple-element.16), channel_id=1, source_target_pairs={{2,0},{4,2},{6,4},{8,6},{10,8},{12,10},{14,12},{16,14},{18,16},{20... | collective-permute-start | bytes 3145736 | tf_op jit(solution)/shard_map/ppermute | solution.py:19
  32.0 1.0 %copy-start.7 = (bf16[4096,128]{1,0:T(8,128)(2,1)}, bf16[4096,128]{1,0:T(8,128)(2,1)S(1)}, u32[]{:S(2)}) copy-start(bf16[4096,128]{1,0:T(8,128)(2,1)S(1)} %collective-permute-done) | copy-start | bytes 3145732

commit v5 on v4

--- a/solution.py
+++ b/solution.py
@@ -335,7 +335,6 @@
         ),
         name="exchange",
     )(far_index[0], outgoing, far_kernel[0], channel_mix)
-    left, back_low = lax.optimization_barrier((left, back_low))
     arrived = shifted(left, "curve", -1)
 
     layer = pl.pallas_call(

time: 48.2 us -> 56.1 us (1.16)
  the two profiles are of different devices: /device:TPU:1 before, /device:TPU:0 now
where the time goes in v5:
time: 56.1 us; the launch traced here: 55.8 us
  Pallas kernels  49.6 us (88%)
  starting transfers between devices  3.85 us (7%)
  local copies, waits for them, and re-layouts  1.58 us (3%)
  between operations  0.76 us (1%)
    pallas_call x1, Pallas kernels, body(): pl.pallas_call(functools.partial(exchange_kernel, groups, shares), out_sh...  26.3 us
    pallas_call x1, Pallas kernels, body(): pl.pallas_call(forward_kernel, out_shape=jax.ShapeDtypeStruct((blocks, pa...  9.11 us
    pallas_call x1, Pallas kernels, body(): pl.pallas_call(backward_kernel, out_shape=(jax.ShapeDtypeStruct((blocks,...  8.63 us
    ppermute x2, starting transfers between devices, shifted(): lax.ppermute(value, axis, [(source, source + steps) for source in range(l...  3.85 us
    pallas_call x1, Pallas kernels, body(): pl.pallas_call(bundle_kernel, out_shape=jax.ShapeDtypeStruct((groups, 2 *...  3.38 us
    pallas_call x1, Pallas kernels, body(): pl.pallas_call(gradient_kernel, out_shape=jax.ShapeDtypeStruct((blocks, p...  2.25 us
    unnamed x16, local copies, waits for them, and re-layouts  1.58 us
  transfers between devices with their start and end apart: 2, of which 0 were waited for; matrix products, arithmetic and copies ran while one was open for 0% of the time, Pallas kernels for 85%

profile of v5, /device:TPU:0, one launch (start us, length us, event | category | flops | bytes accessed | tf_op | source)
XLA Modules:
  0.0 55.8 jit_solution(5823479784371552633)
XLA Ops:
  0.6 2.4 %collective-permute-start = (bf16[4096,128]{1,0:T(8,128)(2,1)}, bf16[4096,128]{1,0:T(8,128)(2,1)S(1)}, u32[]{:S(2)}, u32[]{:S(2)}) collective-permute-start(bf16[4096,128]{1,0:T(8,128)(2,1)} %param.10), channel_id=1, source_target_pairs={{0,2},{2,4},{4,6},{6,8},{8,10},{10,12},{12,14},{14,16},{16,18},{18... | collective-permute-start | bytes 3145736 | tf_op jit(solution)/shard_map/ppermute | solution.py:19
  3.1 3.4 %bundle.1.send_ref = bf16[16,32,128]{2,1,0:T(8,128)(2,1)} custom-call(s32[8]{0:T(128)} %bitcast.11, bf16[32,128,128]{2,1,0:T(8,128)(2,1)} %bitcast.16, bf16[32,128,128]{2,1,0:T(8,128)(2,1)} %bitcast.14, bf16[32,16,128]{2,1,0:T(8,128)(2,1)} %bin_ref.3, bf16[32,16,128]{2,1,0:T(8,128)(2,1)} %bitcast.18, f32[8,16,16]{2,1,0:T(8,128)} %bitcast.9), custom_call_target="tpu_custom_call" | custom-call | tf_op jit(solution)/shard_map/bundle/pallas_call | solution.py:283
  6.4 0.0 copy-start.3
  6.4 0.0 copy-start.4
  6.5 0.0 copy-start.5
  6.5 8.6 %backward.1 = (bf16[32,128,128]{2,1,0:T(8,128)(2,1)}, f32[32,128,128]{2,1,0:T(8,128)}) custom-call(s32[8,32]{1,0:T(8,128)} %bitcast.21, s32[32]{0:T(128)} %count_ref.3, bf16[32,8,128,128]{3,2,1,0:T(8,128)(2,1)} %tile_hbm.3, bf16[32,128,128]{2,1,0:T(8,128)(2,1)} %bitcast.15), custom_call_target="tpu_custom_call" | custom-call | flops 4294967296 | bytes 16777216 | tf_op jit(solution)/shard_map/backward/pallas_call | solution.py:294
  15.1 0.0 copy-start
  15.1 0.0 copy-start.1
  15.1 1.4 %collective-permute-start.1 = (bf16[32,128,128]{2,1,0:T(8,128)(2,1)}, bf16[32,128,128]{2,1,0:T(8,128)(2,1)S(1)}, u32[]{:S(2)}, u32[]{:S(2)}) collective-permute-start(bf16[32,128,128]{2,1,0:T(8,128)(2,1)} %get-tuple-element.12), channel_id=1, source_target_pairs={{2,0},{4,2},{6,4},{8,6},{10,8},{12,10},{14,12},{16,14},{18,16},{20... | collective-permute-start | bytes 3145736 | tf_op jit(solution)/shard_map/ppermute | solution.py:19
  16.6 0.0 copy-done.2
  16.6 0.0 copy-done.3
  16.6 0.0 copy-done.4
  16.6 0.0 copy-done.5
  16.6 26.3 %exchange.1 = (bf16[16,128]{1,0:T(8,128)(2,1)S(1)}, bf16[16,128]{1,0:T(8,128)(2,1)S(1)}) custom-call(s32[8]{0:T(128)S(1)} %bitcast.12, bf16[16,32,128]{2,1,0:T(8,128)(2,1)S(1)} %copy-done.2, f32[8,16,16]{2,1,0:T(8,128)S(1)} %bitcast.10, f32[256,256]{1,0:T(8,128)S(1)} %copy-done.3), custom_call_target="tpu_custom_call" | custom-call | bytes 33554432 | tf_op jit(solution)/shard_map/exchange/pallas_call | solution.py:315
  42.9 0.0 copy-start.6
  42.9 0.6 %copy-done.6 = bf16[16,128]{1,0:T(8,128)(2,1)} copy-done((bf16[16,128]{1,0:T(8,128)(2,1)}, bf16[16,128]{1,0:T(8,128)(2,1)S(1)}, u32[]{:S(2)}) %copy-start.6) | copy-done | bytes 4120
  43.5 0.0 collective-permute-done
  43.5 0.0 copy-start.7
  43.5 1.0 %copy-done.7 = bf16[4096,128]{1,0:T(8,128)(2,1)} copy-done((bf16[4096,128]{1,0:T(8,128)(2,1)}, bf16[4096,128]{1,0:T(8,128)(2,1)S(1)}, u32[]{:S(2)}) %copy-start.7) | copy-done | bytes 1048600
  44.4 9.1 %forward.1 = bf16[32,128,128]{2,1,0:T(8,128)(2,1)} custom-call(s32[8,32]{1,0:T(8,128)} %bitcast.22, s32[32]{0:T(128)} %count_ref.3, bf16[32,8,128,128]{3,2,1,0:T(8,128)(2,1)} %tile_hbm.3, bf16[32,128,128]{2,1,0:T(8,128)(2,1)} %bitcast.20, bf16[32,128,128]{2,1,0:T(8,128)(2,1)} %bitcast.17, bf16[32,16,128]{2,1,0:T(8,128)(2,1)} %bitcast.19, ...), custom_call_target="tpu_custom_call" | custom-call | flops 4294967296 | bytes 16777216 | tf_op jit(solution)/shard_map/forward/pallas_call | solution.py:340
  53.6 0.0 collective-permute-done.1.arrived_ref
  53.6 0.0 copy-done
  53.6 0.0 copy-done.1
  53.6 2.3 %gradient.1 = bf16[32,128,128]{2,1,0:T(8,128)(2,1)} custom-call(f32[32,128,128]{2,1,0:T(8,128)S(1)} %copy-done, bf16[32,128,128]{2,1,0:T(8,128)(2,1)S(1)} %collective-permute-done.1.arrived_ref, bf16[32,16,128]{2,1,0:T(8,128)(2,1)S(1)} %copy-done.1, bf16[16,128]{1,0:T(8,128)(2,1)S(1)} %get-tuple-element.13.back_ref), custom_call_target="tpu_custom_call" | custom-call | tf_op jit(solution)/shard_map/gradient/pallas_call | solution.py:360
  (1 shorter events, 0.0 us)
Async XLA Ops:
  0.6 42.8 %collective-permute-start = (bf16[4096,128]{1,0:T(8,128)(2,1)}, bf16[4096,128]{1,0:T(8,128)(2,1)S(1)}, u32[]{:S(2)}, u32[]{:S(2)}) collective-permute-start(bf16[4096,128]{1,0:T(8,128)(2,1)} %param.10), channel_id=1, source_target_pairs={{0,2},{2,4},{4,6},{6,8},{8,10},{10,12},{12,14},{14,16},{16,18},{18... | collective-permute-start | bytes 3145736 | tf_op jit(solution)/shard_map/ppermute | solution.py:19
  6.4 10.1 %copy-start.2 = (bf16[16,32,128]{2,1,0:T(8,128)(2,1)S(1)}, bf16[16,32,128]{2,1,0:T(8,128)(2,1)}, u32[]{:S(2)}) copy-start(bf16[16,32,128]{2,1,0:T(8,128)(2,1)} %bundle.1.send_ref) | copy-start | bytes 393220
  6.4 10.1 %copy-start.3 = (f32[256,256]{1,0:T(8,128)S(1)}, f32[256,256]{1,0:T(8,128)}, u32[]{:S(2)}) copy-start(f32[256,256]{1,0:T(8,128)} %mix_ref.1) | copy-start | bytes 786436
  6.4 10.1 %copy-start.4 = (f32[1,8,16,16]{3,2,1,0:T(8,128)S(1)}, f32[1,8,16,16]{3,2,1,0:T(8,128)}, u32[]{:S(2)}) copy-start(f32[1,8,16,16]{3,2,1,0:T(8,128)} %param.17) | copy-start | bytes 24580
  6.5 10.1 %copy-start.5 = (s32[1,8]{1,0:T(1,128)S(1)}, s32[1,8]{1,0:T(1,128)}, u32[]{:S(2)}) copy-start(s32[1,8]{1,0:T(1,128)} %param.18) | copy-start | bytes 100
  15.1 38.5 %copy-start = (f32[32,128,128]{2,1,0:T(8,128)S(1)}, f32[32,128,128]{2,1,0:T(8,128)}, u32[]{:S(2)}) copy-start(f32[32,128,128]{2,1,0:T(8,128)} %get-tuple-element.11.own_ref) | copy-start | bytes 6291460
  15.1 38.5 %copy-start.1 = (bf16[32,16,128]{2,1,0:T(8,128)(2,1)S(1)}, bf16[32,16,128]{2,1,0:T(8,128)(2,1)}, u32[]{:S(2)}) copy-start(bf16[32,16,128]{2,1,0:T(8,128)(2,1)} %bin_ref.3) | copy-start | bytes 393220
  15.1 38.4 %collective-permute-start.1 = (bf16[32,128,128]{2,1,0:T(8,128)(2,1)}, bf16[32,128,128]{2,1,0:T(8,128)(2,1)S(1)}, u32[]{:S(2)}, u32[]{:S(2)}) collective-permute-start(bf16[32,128,128]{2,1,0:T(8,128)(2,1)} %get-tuple-element.12), channel_id=1, source_target_pairs={{2,0},{4,2},{6,4},{8,6},{10,8},{12,10},{14,12},{16,14},{18,16},{20... | collective-permute-start | bytes 3145736 | tf_op jit(solution)/shard_map/ppermute | solution.py:19
  42.9 0.6 %copy-start.6 = (bf16[16,128]{1,0:T(8,128)(2,1)}, bf16[16,128]{1,0:T(8,128)(2,1)S(1)}, u32[]{:S(2)}) copy-start(bf16[16,128]{1,0:T(8,128)(2,1)S(1)} %get-tuple-element.10.far_ref) | copy-start | bytes 12292
  43.5 1.0 %copy-start.7 = (bf16[4096,128]{1,0:T(8,128)(2,1)}, bf16[4096,128]{1,0:T(8,128)(2,1)S(1)}, u32[]{:S(2)}) copy-start(bf16[4096,128]{1,0:T(8,128)(2,1)S(1)} %collective-permute-done) | copy-start | bytes 3145732
